TPU v7x, 512 devices: a whole 4x4x16 slice. The times are simulated.
512 devices in a mesh: dp: 32 (over x_hi, z), tensor: 16 (over x_lo, y, core).
Axes of the slice: x: 4 (x_hi: 2, x_lo: 2; x = x_hi * 2 + x_lo), y: 4, z: 16, core: 2. Of those that a mesh axis runs over, the one named last changes fastest.
Arguments:
- hidden_in: bfloat16 [24576, 16384], P('dp', 'tensor'), may hold values from -6 to 6
- kv_grad: bfloat16 [24576, 2048], P('dp', 'tensor'), may hold values from -6 to 6
- frozen_kv: bfloat16 [16384, 2048], P('tensor', 'dp'), may hold values from -0.046875 to 0.046875
- adapter_down: bfloat16 [16384, 64], P('tensor'), may hold values from -0.046875 to 0.046875
- adapter_up: bfloat16 [64, 2048], replicated, may hold values from -0.75 to 0.75
- lengths: int32 [64], P('dp'), may hold values from 1 to 384, 12288 in all
Outputs:
- input_grad: bfloat16 [24576, 16384], P('dp', 'tensor')
- down_grad: float32 [16384, 64], P('tensor')
- up_grad: float32 [64, 2048], P(None, 'tensor')
Inputs may be any that keep to these rules, and one draw needn't show every extreme that they name: lengths of the 64 sequences; the longest fills all 384 slots.
All inputs are finite; a program needn't handle non-finite values. No bound on the sum of `lengths` on one device may be relied on, other than what follows from the above.
Results may differ from a plain program's by a relative error of at most 0.0033.
Values may be sent and summed in bfloat16 or wider, within the bound.
No kernel may reach another device: no remote copies, remote signals or barrier semaphores. Data moves between devices by JAX's collectives and lax.ppermute only.
A program may use at most 64 MiB of HBM per device.

v0:
```python
import jax
import jax.numpy as jnp
from jax import lax
from jax.sharding import PartitionSpec as P


def contract_last(left, right):
    return lax.dot_general(
        left, right, (((1,), (1,)), ((), ())), preferred_element_type=jnp.float32
    )


def contract_first(left, right):
    return lax.dot_general(
        left, right, (((0,), (0,)), ((), ())), preferred_element_type=jnp.float32
    )


def per_device(hidden_in, kv_grad, frozen_kv, adapter_down, adapter_up, lengths):
    rows = hidden_in.shape[0]
    local_seqs = lengths.shape[0]
    slots = rows // local_seqs
    total_seqs = local_seqs * lax.axis_size("dp")
    index_rows = jnp.arange(rows, dtype=jnp.int32)
    position = index_rows % slots
    sequence = index_rows // slots
    picker = sequence[:, None] == jnp.arange(local_seqs, dtype=jnp.int32)[None, :]
    limit = jnp.sum(jnp.where(picker, lengths[None, :], 0), axis=1)
    masked = jnp.where((position < limit)[:, None], kv_grad, jnp.zeros_like(kv_grad))
    partial_low = jnp.dot(hidden_in, adapter_down, preferred_element_type=jnp.float32)
    projected = lax.psum(partial_low, "tensor").astype(jnp.bfloat16)
    up_part = 0.25 / total_seqs * contract_first(projected, masked)
    full_grad = lax.all_gather(masked, "tensor", axis=1, tiled=True)
    coupled = (0.25 * contract_last(full_grad, adapter_up)).astype(jnp.bfloat16)
    initial = contract_last(coupled, adapter_down)
    input_grad = initial + contract_last(
        full_grad, lax.all_gather(frozen_kv, "dp", axis=1, tiled=True)
    )
    down_part = contract_first(hidden_in, coupled) / total_seqs
    down_grad, up_grad = lax.psum((down_part, up_part), "dp")
    return (input_grad.astype(jnp.bfloat16), down_grad, up_grad)


def solution(mesh):
    in_specs = (
        P("dp", "tensor"),
        P("dp", "tensor"),
        P("tensor", "dp"),
        P("tensor", None),
        P(),
        P("dp"),
    )
    out_specs = (P("dp", "tensor"), P("tensor", None), P(None, "tensor"))
    return jax.shard_map(
        per_device, mesh=mesh, in_specs=in_specs, out_specs=out_specs, check_vma=False
    )
```

profile of v0, /device:TPU:8, one launch (start us, length us, event | category | flops | bytes accessed | tf_op | source)
XLA Modules:
  0.0 537.2 jit_solution(975099732829996543)
XLA Ops:
  7.2 0.0 copy-start
  7.2 0.0 copy-start.2
  7.2 0.0 all-gather.3.cloned.1.call-start
  7.3 0.9 fusion.3
  8.1 1.8 broadcast_select_fusion
  9.9 0.0 all-gather.3.cloned.1.call-update
  9.9 0.0 all-gather.5.cloned.1.call-start
  10.0 0.7 all-gather.5.cloned.1.call-update
  10.7 0.0 all-reduce.3.cloned.1.call-start
  10.7 0.0 copy-done
  10.7 1.5 fusion.11
  12.2 58.4 %all-reduce.4 = bf16[768,64]{1,0:T(8,128)(2,1)S(1)} all-reduce(f32[768,64]{1,0:T(8,128)S(1)} %fusion.11), channel_id=1, replica_groups=mesh['dp'=32,'tensor'=16] {'tensor'}, use_global_device_ids=true, to_apply=%region_2.3 | all-reduce | flops 49152 | bytes 294912 | tf_op jit(solution)/shard_map/psum | solution.py:31
  70.6 1.1 convolution_multiply_fusion.2
  71.8 153.3 %psum.23 = f32[64,128]{1,0:T(8,128)} all-reduce(f32[64,128]{1,0:T(8,128)S(1)} %convolution_multiply_fusion.2), channel_id=1, replica_groups=mesh['dp'=32,'tensor'=16] {'dp'}, use_global_device_ids=true, to_apply=%region_3.4 | all-reduce | flops 8192 | bytes 65536 | tf_op jit(solution)/shard_map/psum | solution.py:40
  225.0 0.0 all-gather.3.cloned.1.call-done
  225.0 0.0 copy-done.2
  225.0 3.0 fusion.1
  228.0 1.1 fusion
  229.1 0.0 all-reduce.3.cloned.1.call-update
  229.1 0.0 copy-start.1
  229.2 3.6 all-gather.5.cloned.1.call-done
  232.8 6.1 %fusion.10 = f32[768,1024]{1,0:T(8,128)S(1)} fusion(bf16[768,2048]{1,0:T(8,128)(2,1)} %all-gather.3.cloned.1.call-done, bf16[1024,2048]{0,1:T(8,128)(2,1)} %all-gather.5.cloned.1.call-done), kind=kOutput, calls=%fused_computation.21 | convolution fusion | flops 3221225472 | bytes 10485760 | tf_op jit(solution)/shard_map/dot_general | solution.py:8
  238.9 0.0 copy-done.1
  238.9 1.7 add_convert_fusion
  240.7 288.3 %all-reduce.3.cloned.1.call-done = f32[1024,64]{0,1:T(8,128)} async-done(((f32[1024,64]{0,1:T(8,128)}), f32[1024,64]{0,1:T(8,128)}) %all-reduce.3.cloned.1.call-update) | async-done | bytes 262160 | tf_op jit(solution)/shard_map/psum | solution.py:40
  529.0 1.7 copy.12
  (2 shorter events, 0.0 us)
Async XLA Ops:
  7.2 3.6 copy-start
  7.2 217.9 %copy-start.2 = (bf16[64,2048]{1,0:T(8,128)(2,1)S(1)}, bf16[64,2048]{1,0:T(8,128)(2,1)}, u32[]{:S(2)}) copy-start(bf16[64,2048]{1,0:T(8,128)(2,1)} %param.10) | copy-start | bytes 786436
  7.2 217.9 %all-gather.3.cloned.1.call-start = ((), (), s32[]{:S(2)}) async-start(), calls=%async_computation | async-start | bytes 3342336 | tf_op jit(solution)/shard_map/all_gather | solution.py:33
  9.9 222.9 %all-gather.5.cloned.1.call-start = ((), (), s32[]{:S(2)}) async-start(), calls=%async_computation.1 | async-start | bytes 4325376 | tf_op jit(solution)/shard_map/all_gather | solution.py:37
  10.7 518.3 %all-reduce.3.cloned.1.call-start = ((), (), s32[]{:S(2)}) async-start(), calls=%async_computation.2 | async-start | bytes 524288 | tf_op jit(solution)/shard_map/psum | solution.py:40
  229.1 9.8 %copy-start.1 = (bf16[1024,64]{0,1:T(8,128)(2,1)S(1)}, bf16[1024,64]{0,1:T(8,128)(2,1)}, u32[]{:S(2)}) copy-start(bf16[1024,64]{0,1:T(8,128)(2,1)} %param.9) | copy-start | bytes 393220
Sparse Core Ops, SparseCore 0:
  10.7 53.1 all-gather.2
  67.0 165.7 all-gather.4
  236.3 292.6 all-reduce.2
where the time goes:
time: 537 us
  waiting for transfers between devices  293 us (55%)
  blocking collectives  212 us (39%)
  matrix products  14.5 us (3%)
  between operations  13.8 us (3%)
    psum x1, waiting for transfers between devices, per_device(): down_grad, up_grad = lax.psum((down_part, up_part), 'dp')  288 us
    psum x1, blocking collectives, per_device(): down_grad, up_grad = lax.psum((down_part, up_part), 'dp')  153 us
    psum x1, blocking collectives, per_device(): projected = lax.psum(partial_low, 'tensor').astype(jnp.bfloat16)  58.4 us
    dot_general x3, matrix products, contract_last(): lax.dot_general(left, right, (((1,), (1,)), ((), ())), preferred_element_...  10.8 us
  transfers between devices with their start and end apart: 3, of which 2 were waited for; matrix products, arithmetic and copies ran while one was open for 3% of the time, Pallas kernels for 0%

commit v1 on v0

v1 whole, which is shorter than its diff:
```python
import jax
import jax.numpy as jnp
from jax import lax
from jax.experimental import pallas as pl
from jax.experimental.pallas import tpu as pltpu
from jax.sharding import PartitionSpec as P

NX, NZ = 2, 16
NY, NC = 4, 2
XH_SWAP = [(i, (i + NZ) % (NX * NZ)) for i in range(NX * NZ)]
XH_GROUPS = [[z, z + NZ] for z in range(NZ)]
Z_GROUPS = [[h * NZ + z for z in range(NZ)] for h in range(NX)]
XL_GROUPS = [[i, i + NY * NC] for i in range(NY * NC)]
CORE_SWAP = [(i, i ^ 1) for i in range(2 * NY * NC)]


def y_shift(k):
    return [
        (a * 8 + y * 2 + c, a * 8 + (y + k) % NY * 2 + c)
        for a in range(2)
        for y in range(NY)
        for c in range(NC)
    ]


def dot(left, right, left_dim, right_dim):
    return lax.dot_general(
        left,
        right,
        (((left_dim,), (right_dim,)), ((), ())),
        preferred_element_type=jnp.float32,
    )


def grad_kernel(place, *refs):
    own, other = refs[0:NY], refs[NY : 2 * NY]
    w_ref, low_ref, down_ref, out_ref = refs[2 * NY :]
    y, core = place[0], place[1]
    left, right = [], []
    for r in range(NY):
        source = (y + (NY - r)) % NY
        for a in range(2):
            for side, c in ((own, core), (other, 1 - core)):
                left.append(side[r][a])
                block = w_ref[pl.ds(source * 4 + c * 2, 2), a]
                right.append(block.reshape(128, block.shape[-1]))
    total = jnp.dot(
        jnp.concatenate(left, axis=1),
        jnp.concatenate(right, axis=0),
        preferred_element_type=jnp.float32,
    )
    total += jnp.dot(low_ref[...], down_ref[...], preferred_element_type=jnp.float32)
    out_ref[...] = total.astype(out_ref.dtype)


def input_gradient(place, own, other, w_all, coupled, down_t):
    rows, features, tile = coupled.shape[0], down_t.shape[1], 256
    whole = pl.BlockSpec((2, rows, 128), lambda i, place: (0, 0, 0))
    return pl.pallas_call(
        grad_kernel,
        grid_spec=pltpu.PrefetchScalarGridSpec(
            num_scalar_prefetch=1,
            grid=(features // tile,),
            in_specs=[whole] * (2 * NY)
            + [
                pl.BlockSpec((NZ, NX, 64, tile), lambda i, place: (0, 0, 0, i)),
                pl.BlockSpec((rows, 64), lambda i, place: (0, 0)),
                pl.BlockSpec((64, tile), lambda i, place: (0, i)),
            ],
            out_specs=pl.BlockSpec((rows, tile), lambda i, place: (0, i)),
        ),
        out_shape=jax.ShapeDtypeStruct((rows, features), jnp.bfloat16),
        compiler_params=pltpu.CompilerParams(vmem_limit_bytes=40 * 1024 * 1024),
        cost_estimate=pl.CostEstimate(
            flops=2 * rows * features * 2112, bytes_accessed=9 << 20, transcendentals=0
        ),
    )(place, *own, *other, w_all, coupled, down_t)


def per_device(hidden_in, kv_grad, frozen_kv, adapter_down, adapter_up, lengths):
    rows = hidden_in.shape[0]
    local_seqs = lengths.shape[0]
    slots = rows // local_seqs
    total_seqs = local_seqs * lax.axis_size("dp")
    members = lax.axis_size("tensor")
    me = lax.axis_index("tensor")
    place = jnp.stack([me // 2 % NY, me % 2]).astype(jnp.int32)

    w_pair = lax.all_gather(frozen_kv.T, "dp", axis=0, axis_index_groups=XH_GROUPS)
    w_all = lax.all_gather(w_pair, "dp", axis=0, axis_index_groups=Z_GROUPS)

    position = jnp.arange(slots, dtype=jnp.int32)
    live = (position[None, :] < lengths[:, None]).reshape(rows, 1)
    masked = jnp.where(live, kv_grad, jnp.zeros_like(kv_grad))

    up_mine = lax.dynamic_slice_in_dim(adapter_up, me * 128, 128, axis=1)
    parts = jnp.concatenate(
        [dot(hidden_in, adapter_down, 1, 0), 0.25 * dot(masked, up_mine, 1, 1)], axis=1
    )
    parts = parts.reshape(members, rows // members, 128)
    summed = lax.all_to_all(parts, "tensor", 0, 0).sum(axis=0).astype(jnp.bfloat16)
    spread = jnp.broadcast_to(summed[None], (members,) + summed.shape)
    low_rows = lax.all_to_all(spread, "tensor", 0, 0).reshape(rows, 128)
    projected, coupled = low_rows[:, :64], low_rows[:, 64:]

    down_part = dot(coupled, hidden_in, 0, 0) / total_seqs
    up_part = 0.25 / total_seqs * dot(projected, masked, 0, 0)
    grads = jnp.concatenate([down_part, up_part], axis=1)
    grads = grads.reshape(NZ, 64 // NZ, grads.shape[1])
    share = lax.all_to_all(grads, "dp", 0, 0, axis_index_groups=Z_GROUPS).sum(axis=0)
    share = share + lax.ppermute(share, "dp", XH_SWAP)
    spread = jnp.broadcast_to(share[None], (NZ,) + share.shape)
    grads = lax.all_to_all(spread, "dp", 0, 0, axis_index_groups=Z_GROUPS)
    grads = grads.reshape(64, grads.shape[2])
    down_grad, up_grad = grads[:, : hidden_in.shape[1]].T, grads[:, hidden_in.shape[1] :]

    pair = lax.all_gather(masked, "tensor", axis=0, axis_index_groups=XL_GROUPS)
    own = [pair] + [lax.ppermute(pair, "tensor", y_shift(r)) for r in range(1, NY)]
    other = [lax.ppermute(block, "tensor", CORE_SWAP) for block in own]

    input_grad = input_gradient(place, own, other, w_all, coupled, adapter_down.T)
    return input_grad, down_grad, up_grad


def solution(mesh):
    in_specs = (
        P("dp", "tensor"),
        P("dp", "tensor"),
        P("tensor", "dp"),
        P("tensor", None),
        P(),
        P("dp"),
    )
    out_specs = (P("dp", "tensor"), P("tensor", None), P(None, "tensor"))
    return jax.shard_map(
        per_device, mesh=mesh, in_specs=in_specs, out_specs=out_specs, check_vma=False
    )
```

time: 537 us -> 154 us (0.29)
  the two profiles are of different devices: /device:TPU:8 before, /device:TPU:1 now
where the time goes in v1:
time: 154 us; the launch traced here: 153 us
  blocking collectives  73.5 us (48%)
  starting transfers between devices  40.7 us (26%)
  between operations  14.3 us (9%)
  local copies, waits for them, and re-layouts  9.55 us (6%)
  Pallas kernels  7.41 us (5%)
  waiting for transfers between devices  3.18 us (2%)
  matrix products  2.25 us (1%)
  other arithmetic  2.05 us (1%)
    all_to_all x1, blocking collectives, per_device(): lax.all_to_all(grads, 'dp', 0, 0, axis_index_groups=Z_GROUPS).sum(axis=0)  32.2 us
    ppermute x4, starting transfers between devices, per_device(): other = [lax.ppermute(block, 'tensor', CORE_SWAP) for block in own]  18.4 us
    all_to_all x1, blocking collectives, per_device(): lax.all_to_all(parts, 'tensor', 0, 0).sum(axis=0).astype(jnp.bfloat16)  16.8 us
    all_to_all x1, blocking collectives, per_device(): low_rows = lax.all_to_all(spread, 'tensor', 0, 0).reshape(rows, 128)  10.3 us
    all_to_all x1, starting transfers between devices, per_device(): grads = lax.all_to_all(spread, 'dp', 0, 0, axis_index_groups=Z_GROUPS)  9.36 us
    all_gather x1, blocking collectives, per_device(): lax.all_gather(frozen_kv.T, 'dp', axis=0, axis_index_groups=XH_GROUPS)  8.58 us
    ppermute x3, starting transfers between devices, per_device(): lax.ppermute(pair, 'tensor', y_shift(r))  8.18 us
    pallas_call x1, Pallas kernels, input_gradient(): pl.pallas_call(grad_kernel, grid_spec=pltpu.PrefetchScalarGridSpec(num_sc...  7.41 us
  transfers between devices with their start and end apart: 10, of which 2 were waited for; matrix products, arithmetic and copies ran while one was open for 7% of the time, Pallas kernels for 0%

profile of v1, /device:TPU:1, one launch (start us, length us, event | category | flops | bytes accessed | tf_op | source)
XLA Modules:
  0.0 152.9 jit_solution(6019043927392462728)
XLA Ops:
  7.2 0.0 copy-start
  7.2 0.0 copy-start.1
  7.2 0.0 all-gather.5.cloned.1.call-start
  7.2 8.6 %all-gather.1 = bf16[128,1024]{1,0:T(8,128)(2,1)} all-gather(bf16[64,1024]{1,0:T(8,128)(2,1)} %bitcast.28), channel_id=3, replica_groups={{0,256},{16,272},{32,288},{48,304},{64,320},{80,336},{96,352},{112,368}..., dimensions={0}, use_global_device_ids=true | all-gather | bytes 393216 | tf_op jit(solution)/shard_map/all_gather | solution.py:89
  15.8 0.0 all-gather.5.cloned.1.call-update
  15.8 0.7 iota_compare_fusion
  16.6 1.1 broadcast_select_fusion
  17.7 0.9 convolution_multiply_fusion.1
  18.6 0.0 copy-done
  18.6 0.0 copy-done.1
  18.6 0.6 fusion.4
  19.3 0.2 copy.10
  19.4 16.8 %all_to_all.20 = f32[16,48,128]{2,1,0:T(8,128)S(1)} all-to-all(f32[16,48,128]{2,1,0:T(8,128)S(1)} %bitcast.26), channel_id=1, replica_groups=mesh['dp'=32,'tensor'=16] {'tensor'}, dimensions={0} | all-to-all | bytes 786432 | tf_op jit(solution)/shard_map/all_to_all | solution.py:101
  36.3 10.3 %all_to_all.21 = bf16[16,48,128]{2,1,0:T(8,128)(2,1)S(1)} all-to-all(bf16[16,48,128]{2,1,0:T(8,128)(2,1)S(1)} %broadcast_in_dim.16), channel_id=1, replica_groups=mesh['dp'=32,'tensor'=16] {'tensor'}, dimensions={0} | all-to-all | bytes 393216 | tf_op jit(solution)/shard_map/all_to_all | solution.py:103
  46.6 0.2 convolution_multiply_fusion.2
  46.8 0.5 copy-done.3
  47.3 0.5 convolution_multiply_fusion
  47.8 0.1 reshape.40
  47.9 32.2 %all_to_all.22 = f32[16,4,1152]{2,1,0:T(4,128)S(1)} all-to-all(f32[16,4,1152]{2,1,0:T(4,128)S(1)} %reshape.40), channel_id=1, replica_groups={{0,16,32,48,64,80,96,112,128,144,160,176,192,208,224,240},{256,272,288,..., dimensions={0} | all-to-all | bytes 589824 | tf_op jit(solution)/shard_map/all_to_all | solution.py:110
  80.1 0.1 reduce_sum.19
  80.2 4.7 %collective-permute-start.7 = (f32[4,1152]{1,0:T(4,128)S(1)}, f32[4,1152]{1,0:T(4,128)S(1)}, u32[]{:S(2)}, u32[]{:S(2)}) collective-permute-start(f32[4,1152]{1,0:T(4,128)S(1)} %reduce_sum.19), channel_id=1, source_target_pairs={{0,256},{16,272},{32,288},{48,304},{64,320},{80,336},{96,352},{112... | collective-permute-start | bytes 55304 | tf_op jit(solution)/shard_map/ppermute | solution.py:111
  84.9 1.3 collective-permute-done.7
  86.2 0.8 broadcast_in_dim.28
  87.0 9.4 %all-to-all-start.3 = ((f32[16,4,1152]{2,1,0:T(4,128)}), f32[16,4,1152]{2,1,0:T(4,128)}, u32[]{:S(2)}, u32[]{:S(2)}) async-start(f32[16,4,1152]{2,1,0:T(4,128)} %broadcast_in_dim.28), calls=%async_computation.3 | async-start | bytes 589824 | tf_op jit(solution)/shard_map/all_to_all | solution.py:113
  96.3 5.6 %all-gather = bf16[1536,128]{1,0:T(8,128)(2,1)S(1)} all-gather(bf16[768,128]{1,0:T(8,128)(2,1)S(1)} %broadcast_select_fusion), channel_id=2, replica_groups={{0,8},{1,9},{2,10},{3,11},{4,12},{5,13},{6,14},{7,15},{16,24},{17,25},{..., dimensions={0}, use_global_device_ids=true | all-gather | bytes 589824 | tf_op jit(solution)/shard_map/all_gather | solution.py:117
  101.9 3.2 %collective-permute-start.2 = (bf16[2,768,128]{2,1,0:T(8,128)(2,1)S(1)}, bf16[2,768,128]{2,1,0:T(8,128)(2,1)S(1)}, u32[]{:S(2)}, u32[]{:S(2)}) collective-permute-start(bf16[2,768,128]{2,1,0:T(8,128)(2,1)S(1)} %bitcast.16), channel_id=1, source_target_pairs={{0,6},{1,7},{2,0},{3,1},{4,2},{5,3},{6,4},{7,5},{8,14},{9,15},{10,... | collective-permute-start | bytes 1179656 | tf_op jit(solution)/shard_map/ppermute | solution.py:118
  105.2 3.0 %collective-permute-start.1 = (bf16[2,768,128]{2,1,0:T(8,128)(2,1)S(1)}, bf16[2,768,128]{2,1,0:T(8,128)(2,1)S(1)}, u32[]{:S(2)}, u32[]{:S(2)}) collective-permute-start(bf16[2,768,128]{2,1,0:T(8,128)(2,1)S(1)} %bitcast.17), channel_id=1, source_target_pairs={{0,4},{1,5},{2,6},{3,7},{4,0},{5,1},{6,2},{7,3},{8,12},{9,13},{10,... | collective-permute-start | bytes 1179656 | tf_op jit(solution)/shard_map/ppermute | solution.py:118
  108.2 1.9 %collective-permute-start = (bf16[2,768,128]{2,1,0:T(8,128)(2,1)S(1)}, bf16[2,768,128]{2,1,0:T(8,128)(2,1)S(1)}, u32[]{:S(2)}, u32[]{:S(2)}) collective-permute-start(bf16[2,768,128]{2,1,0:T(8,128)(2,1)S(1)} %bitcast.18), channel_id=1, source_target_pairs={{0,2},{1,3},{2,4},{3,5},{4,6},{5,7},{6,0},{7,1},{8,10},{9,11},{10,... | collective-permute-start | bytes 1179656 | tf_op jit(solution)/shard_map/ppermute | solution.py:118
  110.1 5.2 %collective-permute-start.3 = (bf16[2,768,128]{2,1,0:T(8,128)(2,1)S(1)}, bf16[2,768,128]{2,1,0:T(8,128)(2,1)}, u32[]{:S(2)}, u32[]{:S(2)}) collective-permute-start(bf16[2,768,128]{2,1,0:T(8,128)(2,1)S(1)} %bitcast.19), channel_id=1, source_target_pairs={{0,1},{1,0},{2,3},{3,2},{4,5},{5,4},{6,7},{7,6},{8,9},{9,8},{10,11... | collective-permute-start | bytes 1179656 | tf_op jit(solution)/shard_map/ppermute | solution.py:119
  115.4 0.0 collective-permute-done.2.refs_3_
  115.4 5.5 %collective-permute-start.6 = (bf16[2,768,128]{2,1,0:T(8,128)(2,1)S(1)}, bf16[2,768,128]{2,1,0:T(8,128)(2,1)}, u32[]{:S(2)}, u32[]{:S(2)}) collective-permute-start(bf16[2,768,128]{2,1,0:T(8,128)(2,1)S(1)} %collective-permute-done.2.refs_3_), channel_id=1, source_target_pairs={{0,1},{1,0},{2,3},{3,2},{4,5},{5,4},{6,7},{7,6},{8,9},{9,8},{10,11... | collective-permute-start | bytes 1179656 | tf_op jit(solution)/shard_map/ppermute | solution.py:119
  120.9 0.0 collective-permute-done.1.refs_2_
  120.9 4.6 %collective-permute-start.5 = (bf16[2,768,128]{2,1,0:T(8,128)(2,1)S(1)}, bf16[2,768,128]{2,1,0:T(8,128)(2,1)}, u32[]{:S(2)}, u32[]{:S(2)}) collective-permute-start(bf16[2,768,128]{2,1,0:T(8,128)(2,1)S(1)} %collective-permute-done.1.refs_2_), channel_id=1, source_target_pairs={{0,1},{1,0},{2,3},{3,2},{4,5},{5,4},{6,7},{7,6},{8,9},{9,8},{10,11... | collective-permute-start | bytes 1179656 | tf_op jit(solution)/shard_map/ppermute | solution.py:119
  125.5 1.8 %collective-permute-done.refs_1_ = bf16[2,768,128]{2,1,0:T(8,128)(2,1)S(1)} collective-permute-done((bf16[2,768,128]{2,1,0:T(8,128)(2,1)S(1)}, bf16[2,768,128]{2,1,0:T(8,128)(2,1)S(1)}, u32[]{:S(2)}, u32[]{:S(2)}) %collective-permute-start) | collective-permute-done | bytes 393248 | tf_op jit(solution)/shard_map/ppermute | solution.py:118
  127.4 3.1 %collective-permute-start.4 = (bf16[2,768,128]{2,1,0:T(8,128)(2,1)S(1)}, bf16[2,768,128]{2,1,0:T(8,128)(2,1)}, u32[]{:S(2)}, u32[]{:S(2)}) collective-permute-start(bf16[2,768,128]{2,1,0:T(8,128)(2,1)S(1)} %collective-permute-done.refs_1_), channel_id=1, source_target_pairs={{0,1},{1,0},{2,3},{3,2},{4,5},{5,4},{6,7},{7,6},{8,9},{9,8},{10,11... | collective-permute-start | bytes 1179656 | tf_op jit(solution)/shard_map/ppermute | solution.py:119
  130.5 0.1 pad_add_fusion.place
  130.6 1.0 slice.16.refs_9_
  131.6 0.0 all-to-all-done.3
  131.6 1.8 %reshape.41 = f32[64,1152]{1,0:T(8,128)} reshape(f32[16,4,1152]{2,1,0:T(4,128)} %all-to-all-done.3) | data formatting | bytes 589824 | tf_op jit(solution)/shard_map/reshape | solution.py:114
  133.4 1.4 slice.19
  134.8 1.7 %slice_bitcast_fusion = f32[1024,64]{0,1:T(8,128)} fusion(f32[64,1152]{1,0:T(8,128)} %reshape.41), kind=kLoop, calls=%fused_computation.5 | loop fusion | bytes 524288 | tf_op jit(solution)/shard_map/transpose | solution.py:115
  136.4 0.0 collective-permute-done.3.refs_4_
  136.4 0.0 collective-permute-done.6.refs_7_
  136.4 0.0 collective-permute-done.5.refs_6_
  136.5 0.0 collective-permute-done.4.refs_5_
  136.5 0.0 all-gather.5.cloned.1.call-done
  136.5 2.2 %copy-done.2 = bf16[32,64,1024]{2,1,0:T(8,128)(2,1)S(1)} copy-done((bf16[32,64,1024]{2,1,0:T(8,128)(2,1)S(1)}, bf16[32,64,1024]{2,1,0:T(8,128)(2,1)}, u32[]{:S(2)}) %copy-start.2) | copy-done | bytes 4194328
  138.7 7.4 %shard_map.85 = bf16[768,1024]{1,0:T(8,128)(2,1)} custom-call(s32[2]{0:T(128)S(1)} %pad_add_fusion.place, bf16[2,768,128]{2,1,0:T(8,128)(2,1)S(1)} %bitcast.20, bf16[2,768,128]{2,1,0:T(8,128)(2,1)S(1)} %collective-permute-done.refs_1_, bf16[2,768,128]{2,1,0:T(8,128)(2,1)S(1)} %collective-permute-done.1.refs_2_, ...), custom_call_target="tpu_custom_call" | custom-call | flops 3321888768 | bytes 9437184 | tf_op jit(solution)/shard_map/pallas_call | solution.py:59
  (8 shorter events, 0.1 us)
Async XLA Ops:
  7.2 11.5 %copy-start = (bf16[768,1024]{1,0:T(8,128)(2,1)S(1)}, bf16[768,1024]{1,0:T(8,128)(2,1)}, u32[]{:S(2)}) copy-start(bf16[768,1024]{1,0:T(8,128)(2,1)} %param.6) | copy-start | bytes 4718596
  7.2 11.5 %copy-start.1 = (bf16[1024,64]{0,1:T(8,128)(2,1)S(1)}, bf16[1024,64]{0,1:T(8,128)(2,1)}, u32[]{:S(2)}) copy-start(bf16[1024,64]{0,1:T(8,128)(2,1)} %param.9) | copy-start | bytes 393220
  7.2 129.3 %all-gather.5.cloned.1.call-start = ((), (), s32[]{:S(2)}) async-start(), calls=%async_computation.4 | async-start | bytes 4456448 | tf_op jit(solution)/shard_map/all_gather | solution.py:90
  46.6 0.7 copy-start.3
  80.2 6.0 %collective-permute-start.7 = (f32[4,1152]{1,0:T(4,128)S(1)}, f32[4,1152]{1,0:T(4,128)S(1)}, u32[]{:S(2)}, u32[]{:S(2)}) collective-permute-start(f32[4,1152]{1,0:T(4,128)S(1)} %reduce_sum.19), channel_id=1, source_target_pairs={{0,256},{16,272},{32,288},{48,304},{64,320},{80,336},{96,352},{112... | collective-permute-start | bytes 55304 | tf_op jit(solution)/shard_map/ppermute | solution.py:111
  87.0 44.6 %all-to-all-start.3 = ((f32[16,4,1152]{2,1,0:T(4,128)}), f32[16,4,1152]{2,1,0:T(4,128)}, u32[]{:S(2)}, u32[]{:S(2)}) async-start(f32[16,4,1152]{2,1,0:T(4,128)} %broadcast_in_dim.28), calls=%async_computation.3 | async-start | bytes 589824 | tf_op jit(solution)/shard_map/all_to_all | solution.py:113
  101.9 13.4 %collective-permute-start.2 = (bf16[2,768,128]{2,1,0:T(8,128)(2,1)S(1)}, bf16[2,768,128]{2,1,0:T(8,128)(2,1)S(1)}, u32[]{:S(2)}, u32[]{:S(2)}) collective-permute-start(bf16[2,768,128]{2,1,0:T(8,128)(2,1)S(1)} %bitcast.16), channel_id=1, source_target_pairs={{0,6},{1,7},{2,0},{3,1},{4,2},{5,3},{6,4},{7,5},{8,14},{9,15},{10,... | collective-permute-start | bytes 1179656 | tf_op jit(solution)/shard_map/ppermute | solution.py:118
  105.2 15.7 %collective-permute-start.1 = (bf16[2,768,128]{2,1,0:T(8,128)(2,1)S(1)}, bf16[2,768,128]{2,1,0:T(8,128)(2,1)S(1)}, u32[]{:S(2)}, u32[]{:S(2)}) collective-permute-start(bf16[2,768,128]{2,1,0:T(8,128)(2,1)S(1)} %bitcast.17), channel_id=1, source_target_pairs={{0,4},{1,5},{2,6},{3,7},{4,0},{5,1},{6,2},{7,3},{8,12},{9,13},{10,... | collective-permute-start | bytes 1179656 | tf_op jit(solution)/shard_map/ppermute | solution.py:118
  108.2 19.2 %collective-permute-start = (bf16[2,768,128]{2,1,0:T(8,128)(2,1)S(1)}, bf16[2,768,128]{2,1,0:T(8,128)(2,1)S(1)}, u32[]{:S(2)}, u32[]{:S(2)}) collective-permute-start(bf16[2,768,128]{2,1,0:T(8,128)(2,1)S(1)} %bitcast.18), channel_id=1, source_target_pairs={{0,2},{1,3},{2,4},{3,5},{4,6},{5,7},{6,0},{7,1},{8,10},{9,11},{10,... | collective-permute-start | bytes 1179656 | tf_op jit(solution)/shard_map/ppermute | solution.py:118
  110.1 26.3 %collective-permute-start.3 = (bf16[2,768,128]{2,1,0:T(8,128)(2,1)S(1)}, bf16[2,768,128]{2,1,0:T(8,128)(2,1)}, u32[]{:S(2)}, u32[]{:S(2)}) collective-permute-start(bf16[2,768,128]{2,1,0:T(8,128)(2,1)S(1)} %bitcast.19), channel_id=1, source_target_pairs={{0,1},{1,0},{2,3},{3,2},{4,5},{5,4},{6,7},{7,6},{8,9},{9,8},{10,11... | collective-permute-start | bytes 1179656 | tf_op jit(solution)/shard_map/ppermute | solution.py:119
  115.4 21.1 %collective-permute-start.6 = (bf16[2,768,128]{2,1,0:T(8,128)(2,1)S(1)}, bf16[2,768,128]{2,1,0:T(8,128)(2,1)}, u32[]{:S(2)}, u32[]{:S(2)}) collective-permute-start(bf16[2,768,128]{2,1,0:T(8,128)(2,1)S(1)} %collective-permute-done.2.refs_3_), channel_id=1, source_target_pairs={{0,1},{1,0},{2,3},{3,2},{4,5},{5,4},{6,7},{7,6},{8,9},{9,8},{10,11... | collective-permute-start | bytes 1179656 | tf_op jit(solution)/shard_map/ppermute | solution.py:119
  120.9 15.5 %collective-permute-start.5 = (bf16[2,768,128]{2,1,0:T(8,128)(2,1)S(1)}, bf16[2,768,128]{2,1,0:T(8,128)(2,1)}, u32[]{:S(2)}, u32[]{:S(2)}) collective-permute-start(bf16[2,768,128]{2,1,0:T(8,128)(2,1)S(1)} %collective-permute-done.1.refs_2_), channel_id=1, source_target_pairs={{0,1},{1,0},{2,3},{3,2},{4,5},{5,4},{6,7},{7,6},{8,9},{9,8},{10,11... | collective-permute-start | bytes 1179656 | tf_op jit(solution)/shard_map/ppermute | solution.py:119
  127.4 9.1 %collective-permute-start.4 = (bf16[2,768,128]{2,1,0:T(8,128)(2,1)S(1)}, bf16[2,768,128]{2,1,0:T(8,128)(2,1)}, u32[]{:S(2)}, u32[]{:S(2)}) collective-permute-start(bf16[2,768,128]{2,1,0:T(8,128)(2,1)S(1)} %collective-permute-done.refs_1_), channel_id=1, source_target_pairs={{0,1},{1,0},{2,3},{3,2},{4,5},{5,4},{6,7},{7,6},{8,9},{9,8},{10,11... | collective-permute-start | bytes 1179656 | tf_op jit(solution)/shard_map/ppermute | solution.py:119
  136.5 2.2 %copy-start.2 = (bf16[32,64,1024]{2,1,0:T(8,128)(2,1)S(1)}, bf16[32,64,1024]{2,1,0:T(8,128)(2,1)}, u32[]{:S(2)}) copy-start(bf16[32,64,1024]{2,1,0:T(8,128)(2,1)} %all-gather.5.cloned.1.call-done) | copy-start | bytes 12582916
Sparse Core Ops, SparseCore 0:
  16.0 96.0 all-gather.4

commit v2 on v1

v2 whole, which is shorter than its diff:
```python
import jax
import jax.numpy as jnp
from jax import lax
from jax.experimental import pallas as pl
from jax.experimental.pallas import tpu as pltpu
from jax.sharding import PartitionSpec as P

NX, NZ = 2, 16
NT = 16
NY, NC = 4, 2
XH_SWAP = [(i, (i + NZ) % (NX * NZ)) for i in range(NX * NZ)]
XH_GROUPS = [[z, z + NZ] for z in range(NZ)]
Z_GROUPS = [[h * NZ + z for z in range(NZ)] for h in range(NX)]
XL_SWAP = [(i, i ^ (NY * NC)) for i in range(2 * NY * NC)]
CORE_SWAP = [(i, i ^ 1) for i in range(2 * NY * NC)]


def y_shift(k):
    return [
        (a * 8 + y * 2 + c, a * 8 + (y + k) % NY * 2 + c)
        for a in range(2)
        for y in range(NY)
        for c in range(NC)
    ]


def dot(left, right, left_dim, right_dim):
    return lax.dot_general(
        left,
        right,
        (((left_dim,), (right_dim,)), ((), ())),
        preferred_element_type=jnp.float32,
    )


def grad_kernel(place, *refs):
    own, other = refs[:NY], refs[NY : 2 * NY]
    low_ref, w_hbm, down_ref, out_ref, w_ref, total, sems = refs[2 * NY :]
    x_lo, y, core = place[0], place[1], place[2]
    copies = []
    for r in range(NY):
        source = (y + (NY - r)) % NY * 4
        for k in range(4):
            half = x_lo if k < 2 else 1 - x_lo
            column = core if k % 2 == 0 else 1 - core
            copies.append(
                pltpu.make_async_copy(
                    w_hbm.at[pl.ds(source + column * 2, 2), half],
                    w_ref.at[r, k],
                    sems.at[r * 4 + k],
                )
            )
            copies[-1].start()
    total[...] = jnp.dot(
        low_ref[:, 64:], down_ref[...], preferred_element_type=jnp.float32
    )
    for r in range(NY):
        for k in range(4):
            copies[r * 4 + k].wait()
        left = [own[r][0], other[r][0], own[r][1], other[r][1]]
        total[...] += jnp.dot(
            jnp.concatenate(left, axis=1),
            w_ref[r].reshape(512, w_ref.shape[-1]),
            preferred_element_type=jnp.float32,
        )
    out_ref[...] = total[...].astype(out_ref.dtype)


def input_gradient(place, own, other, low_rows, w_all, down_t):
    rows, features = low_rows.shape[0], down_t.shape[1]
    vmem = pl.BlockSpec(memory_space=pltpu.VMEM)
    return pl.pallas_call(
        grad_kernel,
        grid_spec=pltpu.PrefetchScalarGridSpec(
            num_scalar_prefetch=1,
            in_specs=[vmem] * (2 * NY + 1) + [pl.BlockSpec(memory_space=pltpu.HBM), vmem],
            out_specs=vmem,
            scratch_shapes=[
                pltpu.VMEM((NY, 4, 2, 64, features), jnp.bfloat16),
                pltpu.VMEM((rows, features), jnp.float32),
                pltpu.SemaphoreType.DMA((4 * NY,)),
            ],
        ),
        out_shape=jax.ShapeDtypeStruct((rows, features), jnp.bfloat16),
        compiler_params=pltpu.CompilerParams(vmem_limit_bytes=58 * 1024 * 1024),
        cost_estimate=pl.CostEstimate(
            flops=2 * rows * features * 2112, bytes_accessed=9 << 20, transcendentals=0
        ),
    )(place, *own, *other, low_rows, w_all, down_t)


def per_device(hidden_in, kv_grad, frozen_kv, adapter_down, adapter_up, lengths):
    rows, features = hidden_in.shape
    local_seqs = lengths.shape[0]
    slots = rows // local_seqs
    total_seqs = local_seqs * lax.axis_size("dp")
    me = lax.axis_index("tensor")
    place = jnp.stack([me // 8, me // 2 % NY, me % 2]).astype(jnp.int32)

    position = jnp.arange(slots, dtype=jnp.int32)
    live = (position[None, :] < lengths[:, None]).reshape(rows, 1)
    masked = jnp.where(live, kv_grad, jnp.zeros_like(kv_grad))

    w_pair = lax.all_gather(frozen_kv.T, "dp", axis=0, axis_index_groups=XH_GROUPS)
    w_all = lax.all_gather(w_pair, "dp", axis=0, axis_index_groups=Z_GROUPS)

    up_mine = lax.dynamic_slice_in_dim(adapter_up, me * 128, 128, axis=1)
    parts = jnp.concatenate(
        [dot(hidden_in, adapter_down, 1, 0), 0.25 * dot(masked, up_mine, 1, 1)], axis=1
    )
    parts = parts.reshape(NT, rows // NT, 128)
    parts, w_pair, to_swap = lax.optimization_barrier((parts, w_pair, masked))
    parts = lax.all_to_all(parts, "tensor", 0, 0)
    swapped = lax.ppermute(to_swap, "tensor", XL_SWAP)
    parts, swapped = lax.optimization_barrier((parts, swapped))
    pair = jnp.stack([masked, swapped])
    summed = parts.sum(axis=0).astype(jnp.bfloat16)
    spread = jnp.broadcast_to(summed[None], (NT,) + summed.shape)
    low_rows = lax.all_to_all(spread, "tensor", 0, 0).reshape(rows, 128)
    low_rows, pair = lax.optimization_barrier((low_rows, pair))
    projected, coupled = low_rows[:, :64], low_rows[:, 64:]

    own = [pair] + [lax.ppermute(pair, "tensor", y_shift(r)) for r in range(1, NY)]
    half = features // 2
    down_part = dot(coupled, hidden_in, 0, 0) / total_seqs
    up_part = 0.25 / total_seqs * dot(projected, masked, 0, 0)
    up_part = jnp.concatenate([up_part, jnp.zeros_like(up_part)], axis=1)
    grads = jnp.concatenate(
        [
            down_part.reshape(8, 8, 2, half).swapaxes(1, 2),
            up_part.reshape(8, 8, 2, 128).swapaxes(1, 2),
        ],
        axis=3,
    )
    grads = grads.reshape(NZ, 8, half + 128).astype(jnp.bfloat16)
    grads = lax.all_to_all(grads, "dp", 0, 0, axis_index_groups=Z_GROUPS)
    other = [lax.ppermute(pair, "tensor", CORE_SWAP)]
    grads, own[1], own[3], other[0] = lax.optimization_barrier(
        (grads, own[1], own[3], other[0])
    )

    share = grads.astype(jnp.float32).sum(axis=0)
    share = share + lax.ppermute(share, "dp", XH_SWAP)
    share, own[2] = lax.optimization_barrier((share, own[2]))
    spread = jnp.broadcast_to(share[None], (NZ,) + share.shape)
    grads = lax.all_to_all(spread, "dp", 0, 0, axis_index_groups=Z_GROUPS)
    other += [lax.ppermute(block, "tensor", CORE_SWAP) for block in own[1:]]
    input_grad = input_gradient(place, own, other, low_rows, w_all, adapter_down.T)
    grads, input_grad = lax.optimization_barrier((grads, input_grad))
    grads = grads.reshape(8, 2, 8, half + 128)
    down_grad = grads[..., :half].swapaxes(1, 2).reshape(64, features).T
    up_grad = grads[:, 0, :, half:].reshape(64, 128)
    return input_grad, down_grad, up_grad


def solution(mesh):
    in_specs = (
        P("dp", "tensor"),
        P("dp", "tensor"),
        P("tensor", "dp"),
        P("tensor", None),
        P(),
        P("dp"),
    )
    out_specs = (P("dp", "tensor"), P("tensor", None), P(None, "tensor"))
    return jax.shard_map(
        per_device, mesh=mesh, in_specs=in_specs, out_specs=out_specs, check_vma=False
    )
```

time: 154 us -> 137 us (0.89)
  blocking collectives: 73.5 us -> 8.59 us
  starting transfers between devices: 40.7 us -> 70.8 us
  waiting for transfers between devices: 3.18 us -> 23.6 us
  local copies, waits for them, and re-layouts: 9.55 us -> 3.78 us
  Pallas kernels: 7.41 us -> 9.14 us
    all_to_all x3 -> x0, blocking collectives: 59.3 us -> none  [the longest x1 32.2 us: per_device(): lax.all_to_all(grads, 'dp', 0, 0, axis_index_groups=Z_GROUPS).sum(axis=0)]
    all_to_all x0 -> x3, starting transfers between devices: none -> 26.5 us  [the longest x1 12.2 us: per_device(): grads = lax.all_to_all(grads, 'dp', 0, 0, axis_index_groups=Z_GROUPS)]
    ppermute x4 -> x5, waiting for transfers between devices: 0.01 us -> 8.61 us  [the longest x1 7.6 us: per_device(): swapped = lax.ppermute(to_swap, 'tensor', XL_SWAP)]
    all_to_all x0 -> x3, waiting for transfers between devices: none -> 6.64 us  [the longest x1 6.44 us: per_device(): low_rows = lax.all_to_all(spread, 'tensor', 0, 0).reshape(rows, 128)]
    all_gather x1 -> x0, blocking collectives: 5.6 us -> none  [per_device(): pair = lax.all_gather(masked, 'tensor', axis=0, axis_index_groups=XL_GROUPS)]
    ppermute x3, waiting for transfers between devices: 1.83 us -> 5.62 us  [per_device(): lax.ppermute(pair, 'tensor', y_shift(r))]
    unnamed x8 -> x16, local copies, waits for them, and re-layouts: 2.65 us -> 0.04 us
    all_to_all x1, starting transfers between devices: 9.36 us -> 11.7 us  [per_device(): grads = lax.all_to_all(spread, 'dp', 0, 0, axis_index_groups=Z_GROUPS)]
  transfers between devices with their start and end apart: 10 -> 14, of which waited for: 2 -> 8; matrix products, arithmetic and copies ran while one was open for 7% -> 6% of each run, Pallas kernels for 0% -> 7%
where the time goes in v2:
time: 137 us; the launch traced here: 136 us
  starting transfers between devices  70.8 us (52%)
  waiting for transfers between devices  23.6 us (17%)
  between operations  14.3 us (10%)
  Pallas kernels  9.14 us (7%)
  blocking collectives  8.59 us (6%)
  local copies, waits for them, and re-layouts  3.78 us (3%)
  other arithmetic  3.42 us (2%)
  matrix products  2.25 us (2%)
    ppermute x3, starting transfers between devices, per_device(): other += [lax.ppermute(block, 'tensor', CORE_SWAP) for block in own[1:]]  13.5 us
    all_to_all x1, starting transfers between devices, per_device(): grads = lax.all_to_all(grads, 'dp', 0, 0, axis_index_groups=Z_GROUPS)  12.2 us
    all_to_all x1, starting transfers between devices, per_device(): grads = lax.all_to_all(spread, 'dp', 0, 0, axis_index_groups=Z_GROUPS)  11.7 us
    all_to_all x1, starting transfers between devices, per_device(): parts = lax.all_to_all(parts, 'tensor', 0, 0)  9.22 us
    pallas_call x1, Pallas kernels, input_gradient(): pl.pallas_call(grad_kernel, grid_spec=pltpu.PrefetchScalarGridSpec(num_sc...  9.14 us
    all_gather x1, blocking collectives, per_device(): lax.all_gather(frozen_kv.T, 'dp', axis=0, axis_index_groups=XH_GROUPS)  8.59 us
    ppermute x3, starting transfers between devices, per_device(): lax.ppermute(pair, 'tensor', y_shift(r))  8.41 us
    ppermute x1, waiting for transfers between devices, per_device(): swapped = lax.ppermute(to_swap, 'tensor', XL_SWAP)  7.6 us
  transfers between devices with their start and end apart: 14, of which 8 were waited for; matrix products, arithmetic and copies ran while one was open for 6% of the time, Pallas kernels for 7%

profile of v2, /device:TPU:1, one launch (start us, length us, event | category | flops | bytes accessed | tf_op | source)
XLA Modules:
  0.0 135.8 jit_solution(14086382780148376090)
XLA Ops:
  7.2 0.0 copy-start
  7.2 0.0 copy-start.4
  7.2 0.0 all-gather.4.cloned.1.call-start
  7.2 8.6 %all-gather = bf16[128,1024]{1,0:T(8,128)(2,1)} all-gather(bf16[64,1024]{1,0:T(8,128)(2,1)} %bitcast.42), channel_id=2, replica_groups={{0,256},{16,272},{32,288},{48,304},{64,320},{80,336},{96,352},{112,368}..., dimensions={0}, use_global_device_ids=true | all-gather | bytes 393216 | tf_op jit(solution)/shard_map/all_gather | solution.py:104
  15.8 0.0 all-gather.4.cloned.1.call-update
  15.9 0.7 iota_compare_fusion
  16.6 1.1 broadcast_select_fusion
  17.7 0.9 convolution_multiply_fusion.1
  18.6 0.0 copy-done
  18.7 0.6 fusion.6
  19.2 0.0 copy-start.2
  19.3 0.9 copy.11
  20.2 9.2 %all-to-all-start = ((f32[16,48,128]{2,1,0:T(8,128)}), f32[16,48,128]{2,1,0:T(8,128)S(1)}, u32[]{:S(2)}, u32[]{:S(2)}) async-start(f32[16,48,128]{2,1,0:T(8,128)} %bitcast), calls=%async_computation | async-start | bytes 786432 | tf_op jit(solution)/shard_map/all_to_all | solution.py:113
  29.4 3.3 %collective-permute-start = (bf16[768,128]{1,0:T(8,128)(2,1)S(1)}, bf16[768,128]{1,0:T(8,128)(2,1)S(1)}, u32[]{:S(2)}, u32[]{:S(2)}) collective-permute-start(bf16[768,128]{1,0:T(8,128)(2,1)S(1)} %broadcast_select_fusion), channel_id=1, source_target_pairs={{0,8},{1,9},{2,10},{3,11},{4,12},{5,13},{6,14},{7,15},{8,0},{9,1},... | collective-permute-start | bytes 589832 | tf_op jit(solution)/shard_map/ppermute | solution.py:114
  32.8 7.6 %collective-permute-done = bf16[768,128]{1,0:T(8,128)(2,1)S(1)} collective-permute-done((bf16[768,128]{1,0:T(8,128)(2,1)S(1)}, bf16[768,128]{1,0:T(8,128)(2,1)S(1)}, u32[]{:S(2)}, u32[]{:S(2)}) %collective-permute-start) | collective-permute-done | bytes 196640 | tf_op jit(solution)/shard_map/ppermute | solution.py:114
  40.4 0.0 all-to-all-done
  40.4 0.7 broadcast_in_dim.16
  41.1 5.0 %all-to-all-start.1 = ((bf16[16,48,128]{2,1,0:T(8,128)(2,1)}), bf16[16,48,128]{2,1,0:T(8,128)(2,1)S(1)}, u32[]{:S(2)}, u32[]{:S(2)}) async-start(bf16[16,48,128]{2,1,0:T(8,128)(2,1)} %broadcast_in_dim.16), calls=%async_computation.1 | async-start | bytes 393216 | tf_op jit(solution)/shard_map/all_to_all | solution.py:119
  46.2 0.2 fusion.12
  46.4 6.4 %all-to-all-done.1 = bf16[16,48,128]{2,1,0:T(8,128)(2,1)S(1)} async-done(((bf16[16,48,128]{2,1,0:T(8,128)(2,1)}), bf16[16,48,128]{2,1,0:T(8,128)(2,1)S(1)}, u32[]{:S(2)}, u32[]{:S(2)}) %all-to-all-start.1) | async-done | bytes 196640 | tf_op jit(solution)/shard_map/all_to_all | solution.py:119
  52.8 0.2 fusion.1
  53.1 0.5 fusion
  53.6 0.7 pad_maximum_fusion.2
  54.3 12.2 %all-to-all-start.2 = ((bf16[16,8,640]{2,1,0:T(8,128)(2,1)}), bf16[16,8,640]{2,1,0:T(8,128)(2,1)S(1)}, u32[]{:S(2)}, u32[]{:S(2)}) async-start(bf16[16,8,640]{2,1,0:T(8,128)(2,1)} %bitcast.10), calls=%async_computation.2 | async-start | bytes 327680 | tf_op jit(solution)/shard_map/all_to_all | solution.py:136
  66.5 2.4 %collective-permute-start.1 = (bf16[2,768,128]{2,1,0:T(8,128)(2,1)S(1)}, bf16[2,768,128]{2,1,0:T(8,128)(2,1)S(1)}, u32[]{:S(2)}, u32[]{:S(2)}) collective-permute-start(bf16[2,768,128]{2,1,0:T(8,128)(2,1)S(1)} %pad_maximum_fusion.1.refs_0_), channel_id=1, source_target_pairs={{0,2},{1,3},{2,4},{3,5},{4,6},{5,7},{6,0},{7,1},{8,10},{9,11},{10,... | collective-permute-start | bytes 1179656 | tf_op jit(solution)/shard_map/ppermute | solution.py:123
  68.9 4.1 %collective-permute-start.2 = (bf16[2,768,128]{2,1,0:T(8,128)(2,1)S(1)}, bf16[2,768,128]{2,1,0:T(8,128)(2,1)S(1)}, u32[]{:S(2)}, u32[]{:S(2)}) collective-permute-start(bf16[2,768,128]{2,1,0:T(8,128)(2,1)S(1)} %pad_maximum_fusion.1.refs_0_), channel_id=1, source_target_pairs={{0,6},{1,7},{2,0},{3,1},{4,2},{5,3},{6,4},{7,5},{8,14},{9,15},{10,... | collective-permute-start | bytes 1179656 | tf_op jit(solution)/shard_map/ppermute | solution.py:123
  73.0 3.5 %collective-permute-start.3 = (bf16[2,768,128]{2,1,0:T(8,128)(2,1)S(1)}, bf16[2,768,128]{2,1,0:T(8,128)(2,1)}, u32[]{:S(2)}, u32[]{:S(2)}) collective-permute-start(bf16[2,768,128]{2,1,0:T(8,128)(2,1)S(1)} %pad_maximum_fusion.1.refs_0_), channel_id=1, source_target_pairs={{0,1},{1,0},{2,3},{3,2},{4,5},{5,4},{6,7},{7,6},{8,9},{9,8},{10,11... | collective-permute-start | bytes 1179656 | tf_op jit(solution)/shard_map/ppermute | solution.py:137
  76.6 1.9 %collective-permute-start.5 = (bf16[2,768,128]{2,1,0:T(8,128)(2,1)S(1)}, bf16[2,768,128]{2,1,0:T(8,128)(2,1)}, u32[]{:S(2)}, u32[]{:S(2)}) collective-permute-start(bf16[2,768,128]{2,1,0:T(8,128)(2,1)S(1)} %pad_maximum_fusion.1.refs_0_), channel_id=1, source_target_pairs={{0,4},{1,5},{2,6},{3,7},{4,0},{5,1},{6,2},{7,3},{8,12},{9,13},{10,... | collective-permute-start | bytes 1179656 | tf_op jit(solution)/shard_map/ppermute | solution.py:123
  78.5 0.7 collective-permute-done.1.refs_1_
  79.3 1.7 %collective-permute-done.2.refs_3_ = bf16[2,768,128]{2,1,0:T(8,128)(2,1)S(1)} collective-permute-done((bf16[2,768,128]{2,1,0:T(8,128)(2,1)S(1)}, bf16[2,768,128]{2,1,0:T(8,128)(2,1)S(1)}, u32[]{:S(2)}, u32[]{:S(2)}) %collective-permute-start.2) | collective-permute-done | bytes 393248 | tf_op jit(solution)/shard_map/ppermute | solution.py:123
  80.9 0.0 collective-permute-done.3.refs_4_
  80.9 0.2 all-to-all-done.2
  81.2 3.8 %collective-permute-start.4 = (f32[8,640]{1,0:T(8,128)S(1)}, f32[8,640]{1,0:T(8,128)S(1)}, u32[]{:S(2)}, u32[]{:S(2)}) collective-permute-start(f32[8,640]{1,0:T(8,128)S(1)} %convert_reduce_fusion), channel_id=1, source_target_pairs={{0,256},{16,272},{32,288},{48,304},{64,320},{80,336},{96,352},{112... | collective-permute-start | bytes 61448 | tf_op jit(solution)/shard_map/ppermute | solution.py:143
  84.9 2.7 %collective-permute-done.4 = f32[8,640]{1,0:T(8,128)S(1)} collective-permute-done((f32[8,640]{1,0:T(8,128)S(1)}, f32[8,640]{1,0:T(8,128)S(1)}, u32[]{:S(2)}, u32[]{:S(2)}) %collective-permute-start.4) | collective-permute-done | bytes 20512 | tf_op jit(solution)/shard_map/ppermute | solution.py:143
  87.6 3.2 %collective-permute-done.5.refs_2_ = bf16[2,768,128]{2,1,0:T(8,128)(2,1)} collective-permute-done((bf16[2,768,128]{2,1,0:T(8,128)(2,1)S(1)}, bf16[2,768,128]{2,1,0:T(8,128)(2,1)}, u32[]{:S(2)}, u32[]{:S(2)}) %collective-permute-start.5) | collective-permute-done | bytes 393248 | tf_op jit(solution)/shard_map/ppermute | solution.py:123
  90.8 0.7 broadcast_in_dim.17
  91.6 11.7 %all-to-all-start.3 = ((f32[16,8,640]{2,1,0:T(8,128)}), f32[16,8,640]{2,1,0:T(8,128)S(1)}, u32[]{:S(2)}, u32[]{:S(2)}) async-start(f32[16,8,640]{2,1,0:T(8,128)} %broadcast_in_dim.17), calls=%async_computation.3 | async-start | bytes 655360 | tf_op jit(solution)/shard_map/all_to_all | solution.py:146
  103.3 9.1 %collective-permute-start.6 = (bf16[2,768,128]{2,1,0:T(8,128)(2,1)S(1)}, bf16[2,768,128]{2,1,0:T(8,128)(2,1)S(1)}, u32[]{:S(2)}, u32[]{:S(2)}) collective-permute-start(bf16[2,768,128]{2,1,0:T(8,128)(2,1)S(1)} %collective-permute-done.1.refs_1_), channel_id=1, source_target_pairs={{0,1},{1,0},{2,3},{3,2},{4,5},{5,4},{6,7},{7,6},{8,9},{9,8},{10,11... | collective-permute-start | bytes 1179656 | tf_op jit(solution)/shard_map/ppermute | solution.py:147
  112.4 1.9 %collective-permute-start.8 = (bf16[2,768,128]{2,1,0:T(8,128)(2,1)S(1)}, bf16[2,768,128]{2,1,0:T(8,128)(2,1)}, u32[]{:S(2)}, u32[]{:S(2)}) collective-permute-start(bf16[2,768,128]{2,1,0:T(8,128)(2,1)S(1)} %collective-permute-done.2.refs_3_), channel_id=1, source_target_pairs={{0,1},{1,0},{2,3},{3,2},{4,5},{5,4},{6,7},{7,6},{8,9},{9,8},{10,11... | collective-permute-start | bytes 1179656 | tf_op jit(solution)/shard_map/ppermute | solution.py:147
  114.4 2.4 %collective-permute-start.7 = (bf16[2,768,128]{2,1,0:T(8,128)(2,1)}, bf16[2,768,128]{2,1,0:T(8,128)(2,1)}, u32[]{:S(2)}, u32[]{:S(2)}) collective-permute-start(bf16[2,768,128]{2,1,0:T(8,128)(2,1)} %collective-permute-done.5.refs_2_), channel_id=1, source_target_pairs={{0,1},{1,0},{2,3},{3,2},{4,5},{5,4},{6,7},{7,6},{8,9},{9,8},{10,11... | collective-permute-start | bytes 1179656 | tf_op jit(solution)/shard_map/ppermute | solution.py:147
  116.8 0.6 pad_add_fusion.place
  117.4 0.0 collective-permute-done.6.refs_5_
  117.5 0.0 collective-permute-done.8.refs_7_
  117.5 1.0 collective-permute-done.7.refs_6_
  118.5 9.1 %shard_map.85 = bf16[768,1024]{1,0:T(8,128)(2,1)} custom-call(s32[3]{0:T(128)} %pad_add_fusion.place, bf16[2,768,128]{2,1,0:T(8,128)(2,1)} %copy-done.3, bf16[2,768,128]{2,1,0:T(8,128)(2,1)} %copy-done.5, bf16[2,768,128]{2,1,0:T(8,128)(2,1)} %collective-permute-done.5.refs_2_, bf16[2,768,128]{2,1,0:T(8,128)(2,1)} %copy-done.6, ...), custom_call_target="tpu_custom_call" | custom-call | flops 3321888768 | bytes 9437184 | tf_op jit(solution)/shard_map/pallas_call | solution.py:72
  127.6 0.0 all-to-all-done.3
  127.6 0.7 slice.16
  128.4 0.6 slice_bitcast_fusion
  (20 shorter events, 0.2 us)
Async XLA Ops:
  7.2 11.5 %copy-start = (bf16[768,1024]{1,0:T(8,128)(2,1)S(1)}, bf16[768,1024]{1,0:T(8,128)(2,1)}, u32[]{:S(2)}) copy-start(bf16[768,1024]{1,0:T(8,128)(2,1)} %param.6) | copy-start | bytes 4718596
  7.2 11.5 %copy-start.4 = (bf16[1024,64]{0,1:T(8,128)(2,1)S(1)}, bf16[1024,64]{0,1:T(8,128)(2,1)}, u32[]{:S(2)}) copy-start(bf16[1024,64]{0,1:T(8,128)(2,1)} %param.9) | copy-start | bytes 393220
  7.2 111.3 %all-gather.4.cloned.1.call-start = ((), (), s32[]{:S(2)}) async-start(), calls=%async_computation.4 | async-start | bytes 4456448 | tf_op jit(solution)/shard_map/all_gather | solution.py:105
  19.2 26.9 %copy-start.2 = (bf16[768,128]{1,0:T(8,128)(2,1)S(1)}, bf16[768,128]{1,0:T(8,128)(2,1)}, u32[]{:S(2)}) copy-start(bf16[768,128]{1,0:T(8,128)(2,1)} %param.7) | copy-start | bytes 589828
  20.2 20.2 %all-to-all-start = ((f32[16,48,128]{2,1,0:T(8,128)}), f32[16,48,128]{2,1,0:T(8,128)S(1)}, u32[]{:S(2)}, u32[]{:S(2)}) async-start(f32[16,48,128]{2,1,0:T(8,128)} %bitcast), calls=%async_computation | async-start | bytes 786432 | tf_op jit(solution)/shard_map/all_to_all | solution.py:113
  29.4 10.9 %collective-permute-start = (bf16[768,128]{1,0:T(8,128)(2,1)S(1)}, bf16[768,128]{1,0:T(8,128)(2,1)S(1)}, u32[]{:S(2)}, u32[]{:S(2)}) collective-permute-start(bf16[768,128]{1,0:T(8,128)(2,1)S(1)} %broadcast_select_fusion), channel_id=1, source_target_pairs={{0,8},{1,9},{2,10},{3,11},{4,12},{5,13},{6,14},{7,15},{8,0},{9,1},... | collective-permute-start | bytes 589832 | tf_op jit(solution)/shard_map/ppermute | solution.py:114
  41.1 11.7 %all-to-all-start.1 = ((bf16[16,48,128]{2,1,0:T(8,128)(2,1)}), bf16[16,48,128]{2,1,0:T(8,128)(2,1)S(1)}, u32[]{:S(2)}, u32[]{:S(2)}) async-start(bf16[16,48,128]{2,1,0:T(8,128)(2,1)} %broadcast_in_dim.16), calls=%async_computation.1 | async-start | bytes 393216 | tf_op jit(solution)/shard_map/all_to_all | solution.py:119
  46.4 34.8 %copy-start.3 = (bf16[2,768,128]{2,1,0:T(8,128)(2,1)}, bf16[2,768,128]{2,1,0:T(8,128)(2,1)S(1)}, u32[]{:S(2)}) copy-start(bf16[2,768,128]{2,1,0:T(8,128)(2,1)S(1)} %pad_maximum_fusion.1.refs_0_) | copy-start | bytes 1179652
  52.8 28.3 %copy-start.1 = (bf16[16,48,128]{2,1,0:T(8,128)(2,1)}, bf16[16,48,128]{2,1,0:T(8,128)(2,1)S(1)}, u32[]{:S(2)}) copy-start(bf16[16,48,128]{2,1,0:T(8,128)(2,1)S(1)} %all-to-all-done.1) | copy-start | bytes 589828
  54.3 26.8 %all-to-all-start.2 = ((bf16[16,8,640]{2,1,0:T(8,128)(2,1)}), bf16[16,8,640]{2,1,0:T(8,128)(2,1)S(1)}, u32[]{:S(2)}, u32[]{:S(2)}) async-start(bf16[16,8,640]{2,1,0:T(8,128)(2,1)} %bitcast.10), calls=%async_computation.2 | async-start | bytes 327680 | tf_op jit(solution)/shard_map/all_to_all | solution.py:136
  66.5 12.7 %collective-permute-start.1 = (bf16[2,768,128]{2,1,0:T(8,128)(2,1)S(1)}, bf16[2,768,128]{2,1,0:T(8,128)(2,1)S(1)}, u32[]{:S(2)}, u32[]{:S(2)}) collective-permute-start(bf16[2,768,128]{2,1,0:T(8,128)(2,1)S(1)} %pad_maximum_fusion.1.refs_0_), channel_id=1, source_target_pairs={{0,2},{1,3},{2,4},{3,5},{4,6},{5,7},{6,0},{7,1},{8,10},{9,11},{10,... | collective-permute-start | bytes 1179656 | tf_op jit(solution)/shard_map/ppermute | solution.py:123
  68.9 12.0 %collective-permute-start.2 = (bf16[2,768,128]{2,1,0:T(8,128)(2,1)S(1)}, bf16[2,768,128]{2,1,0:T(8,128)(2,1)S(1)}, u32[]{:S(2)}, u32[]{:S(2)}) collective-permute-start(bf16[2,768,128]{2,1,0:T(8,128)(2,1)S(1)} %pad_maximum_fusion.1.refs_0_), channel_id=1, source_target_pairs={{0,6},{1,7},{2,0},{3,1},{4,2},{5,3},{6,4},{7,5},{8,14},{9,15},{10,... | collective-permute-start | bytes 1179656 | tf_op jit(solution)/shard_map/ppermute | solution.py:123
  73.0 7.9 %collective-permute-start.3 = (bf16[2,768,128]{2,1,0:T(8,128)(2,1)S(1)}, bf16[2,768,128]{2,1,0:T(8,128)(2,1)}, u32[]{:S(2)}, u32[]{:S(2)}) collective-permute-start(bf16[2,768,128]{2,1,0:T(8,128)(2,1)S(1)} %pad_maximum_fusion.1.refs_0_), channel_id=1, source_target_pairs={{0,1},{1,0},{2,3},{3,2},{4,5},{5,4},{6,7},{7,6},{8,9},{9,8},{10,11... | collective-permute-start | bytes 1179656 | tf_op jit(solution)/shard_map/ppermute | solution.py:137
  76.6 14.2 %collective-permute-start.5 = (bf16[2,768,128]{2,1,0:T(8,128)(2,1)S(1)}, bf16[2,768,128]{2,1,0:T(8,128)(2,1)}, u32[]{:S(2)}, u32[]{:S(2)}) collective-permute-start(bf16[2,768,128]{2,1,0:T(8,128)(2,1)S(1)} %pad_maximum_fusion.1.refs_0_), channel_id=1, source_target_pairs={{0,4},{1,5},{2,6},{3,7},{4,0},{5,1},{6,2},{7,3},{8,12},{9,13},{10,... | collective-permute-start | bytes 1179656 | tf_op jit(solution)/shard_map/ppermute | solution.py:123
  79.3 39.2 %copy-start.5 = (bf16[2,768,128]{2,1,0:T(8,128)(2,1)}, bf16[2,768,128]{2,1,0:T(8,128)(2,1)S(1)}, u32[]{:S(2)}) copy-start(bf16[2,768,128]{2,1,0:T(8,128)(2,1)S(1)} %collective-permute-done.1.refs_1_) | copy-start | bytes 1179652
  80.9 37.5 %copy-start.6 = (bf16[2,768,128]{2,1,0:T(8,128)(2,1)}, bf16[2,768,128]{2,1,0:T(8,128)(2,1)S(1)}, u32[]{:S(2)}) copy-start(bf16[2,768,128]{2,1,0:T(8,128)(2,1)S(1)} %collective-permute-done.2.refs_3_) | copy-start | bytes 1179652
  81.2 6.4 %collective-permute-start.4 = (f32[8,640]{1,0:T(8,128)S(1)}, f32[8,640]{1,0:T(8,128)S(1)}, u32[]{:S(2)}, u32[]{:S(2)}) collective-permute-start(f32[8,640]{1,0:T(8,128)S(1)} %convert_reduce_fusion), channel_id=1, source_target_pairs={{0,256},{16,272},{32,288},{48,304},{64,320},{80,336},{96,352},{112... | collective-permute-start | bytes 61448 | tf_op jit(solution)/shard_map/ppermute | solution.py:143
  91.6 36.1 %all-to-all-start.3 = ((f32[16,8,640]{2,1,0:T(8,128)}), f32[16,8,640]{2,1,0:T(8,128)S(1)}, u32[]{:S(2)}, u32[]{:S(2)}) async-start(f32[16,8,640]{2,1,0:T(8,128)} %broadcast_in_dim.17), calls=%async_computation.3 | async-start | bytes 655360 | tf_op jit(solution)/shard_map/all_to_all | solution.py:146
  103.3 14.1 %collective-permute-start.6 = (bf16[2,768,128]{2,1,0:T(8,128)(2,1)S(1)}, bf16[2,768,128]{2,1,0:T(8,128)(2,1)S(1)}, u32[]{:S(2)}, u32[]{:S(2)}) collective-permute-start(bf16[2,768,128]{2,1,0:T(8,128)(2,1)S(1)} %collective-permute-done.1.refs_1_), channel_id=1, source_target_pairs={{0,1},{1,0},{2,3},{3,2},{4,5},{5,4},{6,7},{7,6},{8,9},{9,8},{10,11... | collective-permute-start | bytes 1179656 | tf_op jit(solution)/shard_map/ppermute | solution.py:147
  112.4 5.0 %collective-permute-start.8 = (bf16[2,768,128]{2,1,0:T(8,128)(2,1)S(1)}, bf16[2,768,128]{2,1,0:T(8,128)(2,1)}, u32[]{:S(2)}, u32[]{:S(2)}) collective-permute-start(bf16[2,768,128]{2,1,0:T(8,128)(2,1)S(1)} %collective-permute-done.2.refs_3_), channel_id=1, source_target_pairs={{0,1},{1,0},{2,3},{3,2},{4,5},{5,4},{6,7},{7,6},{8,9},{9,8},{10,11... | collective-permute-start | bytes 1179656 | tf_op jit(solution)/shard_map/ppermute | solution.py:147
  114.4 4.1 %collective-permute-start.7 = (bf16[2,768,128]{2,1,0:T(8,128)(2,1)}, bf16[2,768,128]{2,1,0:T(8,128)(2,1)}, u32[]{:S(2)}, u32[]{:S(2)}) collective-permute-start(bf16[2,768,128]{2,1,0:T(8,128)(2,1)} %collective-permute-done.5.refs_2_), channel_id=1, source_target_pairs={{0,1},{1,0},{2,3},{3,2},{4,5},{5,4},{6,7},{7,6},{8,9},{9,8},{10,11... | collective-permute-start | bytes 1179656 | tf_op jit(solution)/shard_map/ppermute | solution.py:147
  117.4 1.0 copy-start.7
Sparse Core Ops, SparseCore 0:
  16.0 81.3 all-gather.3

commit v3 on v2

--- a/solution.py
+++ b/solution.py
@@ -34,51 +34,72 @@
 
 
 def grad_kernel(place, *refs):
-    own, other = refs[:NY], refs[NY : 2 * NY]
-    low_ref, w_hbm, down_ref, out_ref, w_ref, total, sems = refs[2 * NY :]
+    own, other, refs = refs[:NY], refs[NY : 2 * NY], refs[2 * NY :]
+    (low_ref, w_hbm, down_ref, out_hbm), refs = refs[:4], refs[4:]
+    g_ref, w_ref, total, out_ref, g_sems, w_sems, out_sems = refs
     x_lo, y, core = place[0], place[1], place[2]
+    rows, features = out_ref.shape
     copies = []
     for r in range(NY):
         source = (y + (NY - r)) % NY * 4
         for k in range(4):
             half = x_lo if k < 2 else 1 - x_lo
             column = core if k % 2 == 0 else 1 - core
+            part = w_hbm.at[pl.ds(source + column * 2, 2), half]
+            at = r * 4 + k
+            copies.append(pltpu.make_async_copy(part, w_ref.at[r, k], w_sems.at[at]))
             copies.append(
                 pltpu.make_async_copy(
-                    w_hbm.at[pl.ds(source + column * 2, 2), half],
-                    w_ref.at[r, k],
-                    sems.at[r * 4 + k],
+                    (own, other)[k % 2][r].at[k // 2], g_ref.at[r, k], g_sems.at[at]
                 )
             )
-            copies[-1].start()
+    for copy in copies:
+        copy.start()
     total[...] = jnp.dot(
         low_ref[:, 64:], down_ref[...], preferred_element_type=jnp.float32
     )
+    results = []
     for r in range(NY):
-        for k in range(4):
-            copies[r * 4 + k].wait()
-        left = [own[r][0], other[r][0], own[r][1], other[r][1]]
-        total[...] += jnp.dot(
-            jnp.concatenate(left, axis=1),
-            w_ref[r].reshape(512, w_ref.shape[-1]),
-            preferred_element_type=jnp.float32,
-        )
-    out_ref[...] = total[...].astype(out_ref.dtype)
+        for copy in copies[r * 8 : r * 8 + 8]:
+            copy.wait()
+        right = w_ref[r].reshape(512, features)
+        height = rows if r < NY - 1 else rows // 3
+        for i in range(rows // height):
+            at = pl.ds(i * height, height)
+            left = jnp.concatenate([g_ref[r, k, at, :] for k in range(4)], axis=1)
+            sums = total[at, :] + jnp.dot(left, right, preferred_element_type=jnp.float32)
+            if r < NY - 1:
+                total[at, :] = sums
+            else:
+                out_ref[at, :] = sums.astype(out_ref.dtype)
+                results.append(
+                    pltpu.make_async_copy(
+                        out_ref.at[at], out_hbm.at[at], out_sems.at[i]
+                    )
+                )
+                results[i].start()
+    for copy in results:
+        copy.wait()
 
 
 def input_gradient(place, own, other, low_rows, w_all, down_t):
     rows, features = low_rows.shape[0], down_t.shape[1]
     vmem = pl.BlockSpec(memory_space=pltpu.VMEM)
+    hbm = pl.BlockSpec(memory_space=pltpu.HBM)
     return pl.pallas_call(
         grad_kernel,
         grid_spec=pltpu.PrefetchScalarGridSpec(
             num_scalar_prefetch=1,
-            in_specs=[vmem] * (2 * NY + 1) + [pl.BlockSpec(memory_space=pltpu.HBM), vmem],
-            out_specs=vmem,
+            in_specs=[hbm] * (2 * NY) + [vmem, hbm, vmem],
+            out_specs=hbm,
             scratch_shapes=[
+                pltpu.VMEM((NY, 4, rows, 128), jnp.bfloat16),
                 pltpu.VMEM((NY, 4, 2, 64, features), jnp.bfloat16),
                 pltpu.VMEM((rows, features), jnp.float32),
+                pltpu.VMEM((rows, features), jnp.bfloat16),
                 pltpu.SemaphoreType.DMA((4 * NY,)),
+                pltpu.SemaphoreType.DMA((4 * NY,)),
+                pltpu.SemaphoreType.DMA((3,)),
             ],
         ),
         out_shape=jax.ShapeDtypeStruct((rows, features), jnp.bfloat16),
@@ -97,12 +118,12 @@
     me = lax.axis_index("tensor")
     place = jnp.stack([me // 8, me // 2 % NY, me % 2]).astype(jnp.int32)
 
+    w_pair = lax.all_gather(frozen_kv.T, "dp", axis=0, axis_index_groups=XH_GROUPS)
+    w_all = lax.all_gather(w_pair, "dp", axis=0, axis_index_groups=Z_GROUPS)
+
     position = jnp.arange(slots, dtype=jnp.int32)
     live = (position[None, :] < lengths[:, None]).reshape(rows, 1)
     masked = jnp.where(live, kv_grad, jnp.zeros_like(kv_grad))
-
-    w_pair = lax.all_gather(frozen_kv.T, "dp", axis=0, axis_index_groups=XH_GROUPS)
-    w_all = lax.all_gather(w_pair, "dp", axis=0, axis_index_groups=Z_GROUPS)
 
     up_mine = lax.dynamic_slice_in_dim(adapter_up, me * 128, 128, axis=1)
     parts = jnp.concatenate(
@@ -113,14 +134,16 @@
     parts = lax.all_to_all(parts, "tensor", 0, 0)
     swapped = lax.ppermute(to_swap, "tensor", XL_SWAP)
     parts, swapped = lax.optimization_barrier((parts, swapped))
-    pair = jnp.stack([masked, swapped])
     summed = parts.sum(axis=0).astype(jnp.bfloat16)
     spread = jnp.broadcast_to(summed[None], (NT,) + summed.shape)
     low_rows = lax.all_to_all(spread, "tensor", 0, 0).reshape(rows, 128)
+    pair = jnp.stack([masked, swapped])
     low_rows, pair = lax.optimization_barrier((low_rows, pair))
     projected, coupled = low_rows[:, :64], low_rows[:, 64:]
 
-    own = [pair] + [lax.ppermute(pair, "tensor", y_shift(r)) for r in range(1, NY)]
+    own = [pair, lax.ppermute(pair, "tensor", y_shift(1)), None]
+    own += [lax.ppermute(pair, "tensor", y_shift(-1))]
+    own[2] = lax.ppermute(own[1], "tensor", y_shift(1))
     half = features // 2
     down_part = dot(coupled, hidden_in, 0, 0) / total_seqs
     up_part = 0.25 / total_seqs * dot(projected, masked, 0, 0)
@@ -142,12 +165,12 @@
     share = grads.astype(jnp.float32).sum(axis=0)
     share = share + lax.ppermute(share, "dp", XH_SWAP)
     share, own[2] = lax.optimization_barrier((share, own[2]))
-    spread = jnp.broadcast_to(share[None], (NZ,) + share.shape)
+    spread = jnp.broadcast_to(share.astype(jnp.bfloat16)[None], (NZ,) + share.shape)
     grads = lax.all_to_all(spread, "dp", 0, 0, axis_index_groups=Z_GROUPS)
     other += [lax.ppermute(block, "tensor", CORE_SWAP) for block in own[1:]]
     input_grad = input_gradient(place, own, other, low_rows, w_all, adapter_down.T)
     grads, input_grad = lax.optimization_barrier((grads, input_grad))
-    grads = grads.reshape(8, 2, 8, half + 128)
+    grads = grads.reshape(8, 2, 8, half + 128).astype(jnp.float32)
     down_grad = grads[..., :half].swapaxes(1, 2).reshape(64, features).T
     up_grad = grads[:, 0, :, half:].reshape(64, 128)
     return input_grad, down_grad, up_grad

time: 137 us -> 130 us (0.949)
  the two profiles are of different devices: /device:TPU:1 before, /device:TPU:56 now
where the time goes in v3:
time: 130 us; the launch traced here: 129 us
  starting transfers between devices  61.6 us (47%)
  waiting for transfers between devices  24.9 us (19%)
  between operations  14.3 us (11%)
  blocking collectives  9.16 us (7%)
  Pallas kernels  8.13 us (6%)
  local copies, waits for them, and re-layouts  5.17 us (4%)
  other arithmetic  3.48 us (3%)
  matrix products  2.25 us (2%)
    all_to_all x1, starting transfers between devices, per_device(): grads = lax.all_to_all(grads, 'dp', 0, 0, axis_index_groups=Z_GROUPS)  15.2 us
    all_to_all x1, starting transfers between devices, per_device(): grads = lax.all_to_all(spread, 'dp', 0, 0, axis_index_groups=Z_GROUPS)  9.45 us
    all_gather x1, blocking collectives, per_device(): lax.all_gather(frozen_kv.T, 'dp', axis=0, axis_index_groups=XH_GROUPS)  9.16 us
    pallas_call x1, Pallas kernels, input_gradient(): pl.pallas_call(grad_kernel, grid_spec=pltpu.PrefetchScalarGridSpec(num_sc...  8.13 us
    ppermute x1, waiting for transfers between devices, per_device(): swapped = lax.ppermute(to_swap, 'tensor', XL_SWAP)  7.72 us
    ppermute x3, starting transfers between devices, per_device(): other += [lax.ppermute(block, 'tensor', CORE_SWAP) for block in own[1:]]  6.25 us
    all_to_all x1, waiting for transfers between devices, per_device(): grads = lax.all_to_all(spread, 'dp', 0, 0, axis_index_groups=Z_GROUPS)  5.87 us
    ppermute x1, starting transfers between devices, per_device(): own[2] = lax.ppermute(own[1], 'tensor', y_shift(1))  5.13 us
  transfers between devices with their start and end apart: 14, of which 5 were waited for; matrix products, arithmetic and copies ran while one was open for 6% of the time, Pallas kernels for 6%

profile of v3, /device:TPU:56, one launch (start us, length us, event | category | flops | bytes accessed | tf_op | source)
XLA Modules:
  0.0 128.9 jit_solution(6554606600217987729)
XLA Ops:
  7.2 0.0 copy-start
  7.2 0.0 copy-start.4
  7.2 0.0 all-gather.4.cloned.1.call-start
  7.2 9.2 %all-gather = bf16[128,1024]{1,0:T(8,128)(2,1)} all-gather(bf16[64,1024]{1,0:T(8,128)(2,1)} %bitcast.43), channel_id=2, replica_groups={{0,256},{16,272},{32,288},{48,304},{64,320},{80,336},{96,352},{112,368}..., dimensions={0}, use_global_device_ids=true | all-gather | bytes 393216 | tf_op jit(solution)/shard_map/all_gather | solution.py:121
  16.4 0.0 all-gather.4.cloned.1.call-update
  16.4 0.7 iota_compare_fusion
  17.2 1.1 broadcast_select_fusion
  18.3 0.9 convolution_multiply_fusion.1
  19.2 0.6 fusion.6
  19.8 0.0 copy-start.2
  19.9 0.9 copy.11
  20.8 4.7 %all-to-all-start = ((f32[16,48,128]{2,1,0:T(8,128)}), f32[16,48,128]{2,1,0:T(8,128)S(1)}, u32[]{:S(2)}, u32[]{:S(2)}) async-start(f32[16,48,128]{2,1,0:T(8,128)} %bitcast), calls=%async_computation | async-start | bytes 786432 | tf_op jit(solution)/shard_map/all_to_all | solution.py:134
  25.5 3.4 %collective-permute-start = (bf16[768,128]{1,0:T(8,128)(2,1)S(1)}, bf16[768,128]{1,0:T(8,128)(2,1)S(1)}, u32[]{:S(2)}, u32[]{:S(2)}) collective-permute-start(bf16[768,128]{1,0:T(8,128)(2,1)S(1)} %broadcast_select_fusion), channel_id=1, source_target_pairs={{0,8},{1,9},{2,10},{3,11},{4,12},{5,13},{6,14},{7,15},{8,0},{9,1},... | collective-permute-start | bytes 589832 | tf_op jit(solution)/shard_map/ppermute | solution.py:135
  28.9 7.7 %collective-permute-done = bf16[768,128]{1,0:T(8,128)(2,1)S(1)} collective-permute-done((bf16[768,128]{1,0:T(8,128)(2,1)S(1)}, bf16[768,128]{1,0:T(8,128)(2,1)S(1)}, u32[]{:S(2)}, u32[]{:S(2)}) %collective-permute-start) | collective-permute-done | bytes 196640 | tf_op jit(solution)/shard_map/ppermute | solution.py:135
  36.6 0.0 all-to-all-done
  36.6 0.7 broadcast_in_dim.16
  37.3 4.8 %all-to-all-start.1 = ((bf16[16,48,128]{2,1,0:T(8,128)(2,1)}), bf16[16,48,128]{2,1,0:T(8,128)(2,1)S(1)}, u32[]{:S(2)}, u32[]{:S(2)}) async-start(bf16[16,48,128]{2,1,0:T(8,128)(2,1)} %broadcast_in_dim.16), calls=%async_computation.1 | async-start | bytes 393216 | tf_op jit(solution)/shard_map/all_to_all | solution.py:139
  42.2 0.2 fusion.12
  42.4 5.0 %all-to-all-done.1 = bf16[16,48,128]{2,1,0:T(8,128)(2,1)S(1)} async-done(((bf16[16,48,128]{2,1,0:T(8,128)(2,1)}), bf16[16,48,128]{2,1,0:T(8,128)(2,1)S(1)}, u32[]{:S(2)}, u32[]{:S(2)}) %all-to-all-start.1) | async-done | bytes 196640 | tf_op jit(solution)/shard_map/all_to_all | solution.py:139
  47.4 4.2 %collective-permute-start.1 = (bf16[2,768,128]{2,1,0:T(8,128)(2,1)S(1)}, bf16[2,768,128]{2,1,0:T(8,128)(2,1)S(1)}, u32[]{:S(2)}, u32[]{:S(2)}) collective-permute-start(bf16[2,768,128]{2,1,0:T(8,128)(2,1)S(1)} %pad_maximum_fusion.1.refs_0_), channel_id=1, source_target_pairs={{0,2},{1,3},{2,4},{3,5},{4,6},{5,7},{6,0},{7,1},{8,10},{9,11},{10,... | collective-permute-start | bytes 1179656 | tf_op jit(solution)/shard_map/ppermute | solution.py:144
  51.5 0.2 fusion.1
  51.8 0.5 fusion
  52.3 0.7 pad_maximum_fusion.2
  53.0 15.2 %all-to-all-start.2 = ((bf16[16,8,640]{2,1,0:T(8,128)(2,1)}), bf16[16,8,640]{2,1,0:T(8,128)(2,1)S(1)}, u32[]{:S(2)}, u32[]{:S(2)}) async-start(bf16[16,8,640]{2,1,0:T(8,128)(2,1)} %bitcast.10), calls=%async_computation.2 | async-start | bytes 327680 | tf_op jit(solution)/shard_map/all_to_all | solution.py:159
  68.2 1.9 %collective-permute-start.2 = (bf16[2,768,128]{2,1,0:T(8,128)(2,1)S(1)}, bf16[2,768,128]{2,1,0:T(8,128)(2,1)S(1)}, u32[]{:S(2)}, u32[]{:S(2)}) collective-permute-start(bf16[2,768,128]{2,1,0:T(8,128)(2,1)S(1)} %pad_maximum_fusion.1.refs_0_), channel_id=1, source_target_pairs={{0,6},{1,7},{2,0},{3,1},{4,2},{5,3},{6,4},{7,5},{8,14},{9,15},{10,... | collective-permute-start | bytes 1179656 | tf_op jit(solution)/shard_map/ppermute | solution.py:145
  70.1 1.9 %collective-permute-start.3 = (bf16[2,768,128]{2,1,0:T(8,128)(2,1)S(1)}, bf16[2,768,128]{2,1,0:T(8,128)(2,1)S(1)}, u32[]{:S(2)}, u32[]{:S(2)}) collective-permute-start(bf16[2,768,128]{2,1,0:T(8,128)(2,1)S(1)} %pad_maximum_fusion.1.refs_0_), channel_id=1, source_target_pairs={{0,1},{1,0},{2,3},{3,2},{4,5},{5,4},{6,7},{7,6},{8,9},{9,8},{10,11... | collective-permute-start | bytes 1179656 | tf_op jit(solution)/shard_map/ppermute | solution.py:160
  72.0 0.0 collective-permute-done.1.refs_1_
  72.1 5.1 %collective-permute-start.5 = (bf16[2,768,128]{2,1,0:T(8,128)(2,1)S(1)}, bf16[2,768,128]{2,1,0:T(8,128)(2,1)}, u32[]{:S(2)}, u32[]{:S(2)}) collective-permute-start(bf16[2,768,128]{2,1,0:T(8,128)(2,1)S(1)} %collective-permute-done.1.refs_1_), channel_id=1, source_target_pairs={{0,2},{1,3},{2,4},{3,5},{4,6},{5,7},{6,0},{7,1},{8,10},{9,11},{10,... | collective-permute-start | bytes 1179656 | tf_op jit(solution)/shard_map/ppermute | solution.py:146
  77.2 4.0 %collective-permute-done.2.refs_3_ = bf16[2,768,128]{2,1,0:T(8,128)(2,1)S(1)} collective-permute-done((bf16[2,768,128]{2,1,0:T(8,128)(2,1)S(1)}, bf16[2,768,128]{2,1,0:T(8,128)(2,1)S(1)}, u32[]{:S(2)}, u32[]{:S(2)}) %collective-permute-start.2) | collective-permute-done | bytes 393248 | tf_op jit(solution)/shard_map/ppermute | solution.py:145
  81.2 0.0 collective-permute-done.3.refs_4_
  81.2 0.8 copy-done.7
  82.0 2.3 %all-to-all-done.2 = bf16[16,8,640]{2,1,0:T(8,128)(2,1)S(1)} async-done(((bf16[16,8,640]{2,1,0:T(8,128)(2,1)}), bf16[16,8,640]{2,1,0:T(8,128)(2,1)S(1)}, u32[]{:S(2)}, u32[]{:S(2)}) %all-to-all-start.2) | async-done | bytes 163872 | tf_op jit(solution)/shard_map/all_to_all | solution.py:159
  84.3 4.6 %collective-permute-start.4 = (f32[8,640]{1,0:T(8,128)S(1)}, f32[8,640]{1,0:T(8,128)S(1)}, u32[]{:S(2)}, u32[]{:S(2)}) collective-permute-start(f32[8,640]{1,0:T(8,128)S(1)} %convert_reduce_fusion), channel_id=1, source_target_pairs={{0,256},{16,272},{32,288},{48,304},{64,320},{80,336},{96,352},{112... | collective-permute-start | bytes 61448 | tf_op jit(solution)/shard_map/ppermute | solution.py:166
  88.9 1.9 %collective-permute-start.6 = (bf16[2,768,128]{2,1,0:T(8,128)(2,1)S(1)}, bf16[2,768,128]{2,1,0:T(8,128)(2,1)S(1)}, u32[]{:S(2)}, u32[]{:S(2)}) collective-permute-start(bf16[2,768,128]{2,1,0:T(8,128)(2,1)S(1)} %collective-permute-done.1.refs_1_), channel_id=1, source_target_pairs={{0,1},{1,0},{2,3},{3,2},{4,5},{5,4},{6,7},{7,6},{8,9},{9,8},{10,11... | collective-permute-start | bytes 1179656 | tf_op jit(solution)/shard_map/ppermute | solution.py:170
  90.8 2.4 %collective-permute-start.8 = (bf16[2,768,128]{2,1,0:T(8,128)(2,1)S(1)}, bf16[2,768,128]{2,1,0:T(8,128)(2,1)}, u32[]{:S(2)}, u32[]{:S(2)}) collective-permute-start(bf16[2,768,128]{2,1,0:T(8,128)(2,1)S(1)} %collective-permute-done.2.refs_3_), channel_id=1, source_target_pairs={{0,1},{1,0},{2,3},{3,2},{4,5},{5,4},{6,7},{7,6},{8,9},{9,8},{10,11... | collective-permute-start | bytes 1179656 | tf_op jit(solution)/shard_map/ppermute | solution.py:170
  93.2 0.0 collective-permute-done.4
  93.3 1.9 %collective-permute-start.7 = (bf16[2,768,128]{2,1,0:T(8,128)(2,1)}, bf16[2,768,128]{2,1,0:T(8,128)(2,1)}, u32[]{:S(2)}, u32[]{:S(2)}) collective-permute-start(bf16[2,768,128]{2,1,0:T(8,128)(2,1)} %collective-permute-done.5.refs_2_), channel_id=1, source_target_pairs={{0,1},{1,0},{2,3},{3,2},{4,5},{5,4},{6,7},{7,6},{8,9},{9,8},{10,11... | collective-permute-start | bytes 1179656 | tf_op jit(solution)/shard_map/ppermute | solution.py:170
  95.2 0.7 broadcast_in_dim.17
  95.9 9.4 %all-to-all-start.3 = ((bf16[16,8,640]{2,1,0:T(8,128)(2,1)}), bf16[16,8,640]{2,1,0:T(8,128)(2,1)S(1)}, u32[]{:S(2)}, u32[]{:S(2)}) async-start(bf16[16,8,640]{2,1,0:T(8,128)(2,1)} %broadcast_in_dim.17), calls=%async_computation.3 | async-start | bytes 327680 | tf_op jit(solution)/shard_map/all_to_all | solution.py:169
  105.3 0.7 pad_add_fusion.place
  106.0 0.0 collective-permute-done.6.refs_5_
  106.0 0.0 collective-permute-done.8.refs_7_
  106.0 0.0 all-gather.4.cloned.1.call-done
  106.0 0.7 copy-done.8
  106.7 8.1 %shard_map.85 = bf16[768,1024]{1,0:T(8,128)(2,1)} custom-call(s32[3]{0:T(128)} %pad_add_fusion.place, bf16[2,768,128]{2,1,0:T(8,128)(2,1)} %copy-done.3, bf16[2,768,128]{2,1,0:T(8,128)(2,1)} %copy-done.5, bf16[2,768,128]{2,1,0:T(8,128)(2,1)} %collective-permute-done.5.refs_2_, bf16[2,768,128]{2,1,0:T(8,128)(2,1)} %copy-done.6, ...), custom_call_target="tpu_custom_call" | custom-call | flops 3321888768 | bytes 9437184 | tf_op jit(solution)/shard_map/pallas_call | solution.py:89
  114.8 5.9 %all-to-all-done.3 = bf16[16,8,640]{2,1,0:T(8,128)(2,1)S(1)} async-done(((bf16[16,8,640]{2,1,0:T(8,128)(2,1)}), bf16[16,8,640]{2,1,0:T(8,128)(2,1)S(1)}, u32[]{:S(2)}, u32[]{:S(2)}) %all-to-all-start.3) | async-done | bytes 163872 | tf_op jit(solution)/shard_map/all_to_all | solution.py:169
  120.7 0.7 slice.16
  121.5 0.6 slice_bitcast_fusion
  (23 shorter events, 0.2 us)
Async XLA Ops:
  7.2 12.0 %copy-start = (bf16[768,1024]{1,0:T(8,128)(2,1)S(1)}, bf16[768,1024]{1,0:T(8,128)(2,1)}, u32[]{:S(2)}) copy-start(bf16[768,1024]{1,0:T(8,128)(2,1)} %param.6) | copy-start | bytes 4718596
  7.2 12.0 %copy-start.4 = (bf16[1024,64]{0,1:T(8,128)(2,1)S(1)}, bf16[1024,64]{0,1:T(8,128)(2,1)}, u32[]{:S(2)}) copy-start(bf16[1024,64]{0,1:T(8,128)(2,1)} %param.9) | copy-start | bytes 393220
  7.2 98.8 %all-gather.4.cloned.1.call-start = ((), (), s32[]{:S(2)}) async-start(), calls=%async_computation.4 | async-start | bytes 4456448 | tf_op jit(solution)/shard_map/all_gather | solution.py:122
  19.8 22.4 %copy-start.2 = (bf16[768,128]{1,0:T(8,128)(2,1)S(1)}, bf16[768,128]{1,0:T(8,128)(2,1)}, u32[]{:S(2)}) copy-start(bf16[768,128]{1,0:T(8,128)(2,1)} %param.7) | copy-start | bytes 589828
  20.8 15.8 %all-to-all-start = ((f32[16,48,128]{2,1,0:T(8,128)}), f32[16,48,128]{2,1,0:T(8,128)S(1)}, u32[]{:S(2)}, u32[]{:S(2)}) async-start(f32[16,48,128]{2,1,0:T(8,128)} %bitcast), calls=%async_computation | async-start | bytes 786432 | tf_op jit(solution)/shard_map/all_to_all | solution.py:134
  25.5 11.1 %collective-permute-start = (bf16[768,128]{1,0:T(8,128)(2,1)S(1)}, bf16[768,128]{1,0:T(8,128)(2,1)S(1)}, u32[]{:S(2)}, u32[]{:S(2)}) collective-permute-start(bf16[768,128]{1,0:T(8,128)(2,1)S(1)} %broadcast_select_fusion), channel_id=1, source_target_pairs={{0,8},{1,9},{2,10},{3,11},{4,12},{5,13},{6,14},{7,15},{8,0},{9,1},... | collective-permute-start | bytes 589832 | tf_op jit(solution)/shard_map/ppermute | solution.py:135
  37.3 10.0 %all-to-all-start.1 = ((bf16[16,48,128]{2,1,0:T(8,128)(2,1)}), bf16[16,48,128]{2,1,0:T(8,128)(2,1)S(1)}, u32[]{:S(2)}, u32[]{:S(2)}) async-start(bf16[16,48,128]{2,1,0:T(8,128)(2,1)} %broadcast_in_dim.16), calls=%async_computation.1 | async-start | bytes 393216 | tf_op jit(solution)/shard_map/all_to_all | solution.py:139
  42.4 41.9 %copy-start.3 = (bf16[2,768,128]{2,1,0:T(8,128)(2,1)}, bf16[2,768,128]{2,1,0:T(8,128)(2,1)S(1)}, u32[]{:S(2)}) copy-start(bf16[2,768,128]{2,1,0:T(8,128)(2,1)S(1)} %pad_maximum_fusion.1.refs_0_) | copy-start | bytes 1179652
  47.4 36.9 %copy-start.1 = (bf16[16,48,128]{2,1,0:T(8,128)(2,1)}, bf16[16,48,128]{2,1,0:T(8,128)(2,1)S(1)}, u32[]{:S(2)}) copy-start(bf16[16,48,128]{2,1,0:T(8,128)(2,1)S(1)} %all-to-all-done.1) | copy-start | bytes 589828
  47.4 24.7 %collective-permute-start.1 = (bf16[2,768,128]{2,1,0:T(8,128)(2,1)S(1)}, bf16[2,768,128]{2,1,0:T(8,128)(2,1)S(1)}, u32[]{:S(2)}, u32[]{:S(2)}) collective-permute-start(bf16[2,768,128]{2,1,0:T(8,128)(2,1)S(1)} %pad_maximum_fusion.1.refs_0_), channel_id=1, source_target_pairs={{0,2},{1,3},{2,4},{3,5},{4,6},{5,7},{6,0},{7,1},{8,10},{9,11},{10,... | collective-permute-start | bytes 1179656 | tf_op jit(solution)/shard_map/ppermute | solution.py:144
  53.0 31.3 %all-to-all-start.2 = ((bf16[16,8,640]{2,1,0:T(8,128)(2,1)}), bf16[16,8,640]{2,1,0:T(8,128)(2,1)S(1)}, u32[]{:S(2)}, u32[]{:S(2)}) async-start(bf16[16,8,640]{2,1,0:T(8,128)(2,1)} %bitcast.10), calls=%async_computation.2 | async-start | bytes 327680 | tf_op jit(solution)/shard_map/all_to_all | solution.py:159
  68.2 13.0 %collective-permute-start.2 = (bf16[2,768,128]{2,1,0:T(8,128)(2,1)S(1)}, bf16[2,768,128]{2,1,0:T(8,128)(2,1)S(1)}, u32[]{:S(2)}, u32[]{:S(2)}) collective-permute-start(bf16[2,768,128]{2,1,0:T(8,128)(2,1)S(1)} %pad_maximum_fusion.1.refs_0_), channel_id=1, source_target_pairs={{0,6},{1,7},{2,0},{3,1},{4,2},{5,3},{6,4},{7,5},{8,14},{9,15},{10,... | collective-permute-start | bytes 1179656 | tf_op jit(solution)/shard_map/ppermute | solution.py:145
  70.1 11.1 %collective-permute-start.3 = (bf16[2,768,128]{2,1,0:T(8,128)(2,1)S(1)}, bf16[2,768,128]{2,1,0:T(8,128)(2,1)S(1)}, u32[]{:S(2)}, u32[]{:S(2)}) collective-permute-start(bf16[2,768,128]{2,1,0:T(8,128)(2,1)S(1)} %pad_maximum_fusion.1.refs_0_), channel_id=1, source_target_pairs={{0,1},{1,0},{2,3},{3,2},{4,5},{5,4},{6,7},{7,6},{8,9},{9,8},{10,11... | collective-permute-start | bytes 1179656 | tf_op jit(solution)/shard_map/ppermute | solution.py:160
  72.1 34.0 %copy-start.5 = (bf16[2,768,128]{2,1,0:T(8,128)(2,1)}, bf16[2,768,128]{2,1,0:T(8,128)(2,1)S(1)}, u32[]{:S(2)}) copy-start(bf16[2,768,128]{2,1,0:T(8,128)(2,1)S(1)} %collective-permute-done.1.refs_1_) | copy-start | bytes 1179652
  72.1 21.2 %collective-permute-start.5 = (bf16[2,768,128]{2,1,0:T(8,128)(2,1)S(1)}, bf16[2,768,128]{2,1,0:T(8,128)(2,1)}, u32[]{:S(2)}, u32[]{:S(2)}) collective-permute-start(bf16[2,768,128]{2,1,0:T(8,128)(2,1)S(1)} %collective-permute-done.1.refs_1_), channel_id=1, source_target_pairs={{0,2},{1,3},{2,4},{3,5},{4,6},{5,7},{6,0},{7,1},{8,10},{9,11},{10,... | collective-permute-start | bytes 1179656 | tf_op jit(solution)/shard_map/ppermute | solution.py:146
  81.2 24.8 %copy-start.6 = (bf16[2,768,128]{2,1,0:T(8,128)(2,1)}, bf16[2,768,128]{2,1,0:T(8,128)(2,1)S(1)}, u32[]{:S(2)}) copy-start(bf16[2,768,128]{2,1,0:T(8,128)(2,1)S(1)} %collective-permute-done.2.refs_3_) | copy-start | bytes 1179652
  81.2 0.8 copy-start.7
  84.3 8.9 %collective-permute-start.4 = (f32[8,640]{1,0:T(8,128)S(1)}, f32[8,640]{1,0:T(8,128)S(1)}, u32[]{:S(2)}, u32[]{:S(2)}) collective-permute-start(f32[8,640]{1,0:T(8,128)S(1)} %convert_reduce_fusion), channel_id=1, source_target_pairs={{0,256},{16,272},{32,288},{48,304},{64,320},{80,336},{96,352},{112... | collective-permute-start | bytes 61448 | tf_op jit(solution)/shard_map/ppermute | solution.py:166
  88.9 17.1 %collective-permute-start.6 = (bf16[2,768,128]{2,1,0:T(8,128)(2,1)S(1)}, bf16[2,768,128]{2,1,0:T(8,128)(2,1)S(1)}, u32[]{:S(2)}, u32[]{:S(2)}) collective-permute-start(bf16[2,768,128]{2,1,0:T(8,128)(2,1)S(1)} %collective-permute-done.1.refs_1_), channel_id=1, source_target_pairs={{0,1},{1,0},{2,3},{3,2},{4,5},{5,4},{6,7},{7,6},{8,9},{9,8},{10,11... | collective-permute-start | bytes 1179656 | tf_op jit(solution)/shard_map/ppermute | solution.py:170
  90.8 15.2 %collective-permute-start.8 = (bf16[2,768,128]{2,1,0:T(8,128)(2,1)S(1)}, bf16[2,768,128]{2,1,0:T(8,128)(2,1)}, u32[]{:S(2)}, u32[]{:S(2)}) collective-permute-start(bf16[2,768,128]{2,1,0:T(8,128)(2,1)S(1)} %collective-permute-done.2.refs_3_), channel_id=1, source_target_pairs={{0,1},{1,0},{2,3},{3,2},{4,5},{5,4},{6,7},{7,6},{8,9},{9,8},{10,11... | collective-permute-start | bytes 1179656 | tf_op jit(solution)/shard_map/ppermute | solution.py:170
  93.3 12.7 %collective-permute-start.7 = (bf16[2,768,128]{2,1,0:T(8,128)(2,1)}, bf16[2,768,128]{2,1,0:T(8,128)(2,1)}, u32[]{:S(2)}, u32[]{:S(2)}) collective-permute-start(bf16[2,768,128]{2,1,0:T(8,128)(2,1)} %collective-permute-done.5.refs_2_), channel_id=1, source_target_pairs={{0,1},{1,0},{2,3},{3,2},{4,5},{5,4},{6,7},{7,6},{8,9},{9,8},{10,11... | collective-permute-start | bytes 1179656 | tf_op jit(solution)/shard_map/ppermute | solution.py:170
  95.9 24.9 %all-to-all-start.3 = ((bf16[16,8,640]{2,1,0:T(8,128)(2,1)}), bf16[16,8,640]{2,1,0:T(8,128)(2,1)S(1)}, u32[]{:S(2)}, u32[]{:S(2)}) async-start(bf16[16,8,640]{2,1,0:T(8,128)(2,1)} %broadcast_in_dim.17), calls=%async_computation.3 | async-start | bytes 327680 | tf_op jit(solution)/shard_map/all_to_all | solution.py:169
  106.0 0.7 copy-start.8
Sparse Core Ops, SparseCore 0:
  16.5 87.0 all-gather.3

commit v4 on v3

--- a/solution.py
+++ b/solution.py
@@ -34,7 +34,7 @@
 
 
 def grad_kernel(place, *refs):
-    own, other, refs = refs[:NY], refs[NY : 2 * NY], refs[2 * NY :]
+    blocks, refs = refs[:NY], refs[NY:]
     (low_ref, w_hbm, down_ref, out_hbm), refs = refs[:4], refs[4:]
     g_ref, w_ref, total, out_ref, g_sems, w_sems, out_sems = refs
     x_lo, y, core = place[0], place[1], place[2]
@@ -50,7 +50,7 @@
             copies.append(pltpu.make_async_copy(part, w_ref.at[r, k], w_sems.at[at]))
             copies.append(
                 pltpu.make_async_copy(
-                    (own, other)[k % 2][r].at[k // 2], g_ref.at[r, k], g_sems.at[at]
+                    blocks[r].at[k % 2, k // 2], g_ref.at[r, k], g_sems.at[at]
                 )
             )
     for copy in copies:
@@ -82,7 +82,7 @@
         copy.wait()
 
 
-def input_gradient(place, own, other, low_rows, w_all, down_t):
+def input_gradient(place, blocks, low_rows, w_all, down_t):
     rows, features = low_rows.shape[0], down_t.shape[1]
     vmem = pl.BlockSpec(memory_space=pltpu.VMEM)
     hbm = pl.BlockSpec(memory_space=pltpu.HBM)
@@ -90,7 +90,7 @@
         grad_kernel,
         grid_spec=pltpu.PrefetchScalarGridSpec(
             num_scalar_prefetch=1,
-            in_specs=[hbm] * (2 * NY) + [vmem, hbm, vmem],
+            in_specs=[hbm] * NY + [vmem, hbm, vmem],
             out_specs=hbm,
             scratch_shapes=[
                 pltpu.VMEM((NY, 4, rows, 128), jnp.bfloat16),
@@ -107,7 +107,7 @@
         cost_estimate=pl.CostEstimate(
             flops=2 * rows * features * 2112, bytes_accessed=9 << 20, transcendentals=0
         ),
-    )(place, *own, *other, low_rows, w_all, down_t)
+    )(place, *blocks, low_rows, w_all, down_t)
 
 
 def per_device(hidden_in, kv_grad, frozen_kv, adapter_down, adapter_up, lengths):
@@ -136,18 +136,17 @@
     parts, swapped = lax.optimization_barrier((parts, swapped))
     summed = parts.sum(axis=0).astype(jnp.bfloat16)
     spread = jnp.broadcast_to(summed[None], (NT,) + summed.shape)
+    pair = jnp.stack([masked, swapped])
+    spread, pair = lax.optimization_barrier((spread, pair))
     low_rows = lax.all_to_all(spread, "tensor", 0, 0).reshape(rows, 128)
-    pair = jnp.stack([masked, swapped])
-    low_rows, pair = lax.optimization_barrier((low_rows, pair))
+    pair_other = lax.ppermute(pair, "tensor", CORE_SWAP)
+    low_rows, pair_other = lax.optimization_barrier((low_rows, pair_other))
     projected, coupled = low_rows[:, :64], low_rows[:, 64:]
 
-    own = [pair, lax.ppermute(pair, "tensor", y_shift(1)), None]
-    own += [lax.ppermute(pair, "tensor", y_shift(-1))]
-    own[2] = lax.ppermute(own[1], "tensor", y_shift(1))
     half = features // 2
     down_part = dot(coupled, hidden_in, 0, 0) / total_seqs
     up_part = 0.25 / total_seqs * dot(projected, masked, 0, 0)
-    up_part = jnp.concatenate([up_part, jnp.zeros_like(up_part)], axis=1)
+    up_part = jnp.pad(up_part, ((0, 0), (0, 128)))
     grads = jnp.concatenate(
         [
             down_part.reshape(8, 8, 2, half).swapaxes(1, 2),
@@ -156,19 +155,20 @@
         axis=3,
     )
     grads = grads.reshape(NZ, 8, half + 128).astype(jnp.bfloat16)
+    grads, pair, pair_other = lax.optimization_barrier((grads, pair, pair_other))
     grads = lax.all_to_all(grads, "dp", 0, 0, axis_index_groups=Z_GROUPS)
-    other = [lax.ppermute(pair, "tensor", CORE_SWAP)]
-    grads, own[1], own[3], other[0] = lax.optimization_barrier(
-        (grads, own[1], own[3], other[0])
-    )
+    block = jnp.stack([pair, pair_other])
+    blocks = [block, lax.ppermute(block, "tensor", y_shift(1)), None]
+    blocks += [lax.ppermute(block, "tensor", y_shift(-1))]
+    blocks[2] = lax.ppermute(blocks[1], "tensor", y_shift(1))
+    grads, blocks[1] = lax.optimization_barrier((grads, blocks[1]))
 
     share = grads.astype(jnp.float32).sum(axis=0)
     share = share + lax.ppermute(share, "dp", XH_SWAP)
-    share, own[2] = lax.optimization_barrier((share, own[2]))
+    share, blocks[3] = lax.optimization_barrier((share, blocks[3]))
     spread = jnp.broadcast_to(share.astype(jnp.bfloat16)[None], (NZ,) + share.shape)
     grads = lax.all_to_all(spread, "dp", 0, 0, axis_index_groups=Z_GROUPS)
-    other += [lax.ppermute(block, "tensor", CORE_SWAP) for block in own[1:]]
-    input_grad = input_gradient(place, own, other, low_rows, w_all, adapter_down.T)
+    input_grad = input_gradient(place, blocks, low_rows, w_all, adapter_down.T)
     grads, input_grad = lax.optimization_barrier((grads, input_grad))
     grads = grads.reshape(8, 2, 8, half + 128).astype(jnp.float32)
     down_grad = grads[..., :half].swapaxes(1, 2).reshape(64, features).T

time: 130 us -> 127 us (0.977)
  the two profiles are of different devices: /device:TPU:56 before, /device:TPU:2 now
where the time goes in v4:
time: 127 us; the launch traced here: 126 us
  starting transfers between devices  43.3 us (34%)
  waiting for transfers between devices  31.2 us (25%)
  blocking collectives  20.3 us (16%)
  between operations  14.3 us (11%)
  Pallas kernels  8.17 us (6%)
  other arithmetic  3.51 us (3%)
  local copies, waits for them, and re-layouts  3.02 us (2%)
  matrix products  2.25 us (2%)
    all_to_all x1, starting transfers between devices, per_device(): grads = lax.all_to_all(grads, 'dp', 0, 0, axis_index_groups=Z_GROUPS)  12.5 us
    all_to_all x1, blocking collectives, per_device(): low_rows = lax.all_to_all(spread, 'tensor', 0, 0).reshape(rows, 128)  12 us
    all_to_all x1, waiting for transfers between devices, per_device(): grads = lax.all_to_all(grads, 'dp', 0, 0, axis_index_groups=Z_GROUPS)  11.8 us
    all_to_all x1, starting transfers between devices, per_device(): parts = lax.all_to_all(parts, 'tensor', 0, 0)  8.63 us
    all_gather x1, blocking collectives, per_device(): lax.all_gather(frozen_kv.T, 'dp', axis=0, axis_index_groups=XH_GROUPS)  8.26 us
    pallas_call x1, Pallas kernels, input_gradient(): pl.pallas_call(grad_kernel, grid_spec=pltpu.PrefetchScalarGridSpec(num_sc...  8.17 us
    ppermute x1, waiting for transfers between devices, per_device(): swapped = lax.ppermute(to_swap, 'tensor', XL_SWAP)  7.67 us
    all_to_all x1, waiting for transfers between devices, per_device(): grads = lax.all_to_all(spread, 'dp', 0, 0, axis_index_groups=Z_GROUPS)  5.59 us
  transfers between devices with their start and end apart: 10, of which 6 were waited for; matrix products, arithmetic and copies ran while one was open for 6% of the time, Pallas kernels for 6%

profile of v4, /device:TPU:2, one launch (start us, length us, event | category | flops | bytes accessed | tf_op | source)
XLA Modules:
  0.0 126.1 jit_solution(10324150688585799395)
XLA Ops:
  7.2 0.0 copy-start
  7.2 0.0 copy-start.4
  7.2 0.0 all-gather.4.cloned.1.call-start
  7.2 8.3 %all-gather = bf16[128,1024]{1,0:T(8,128)(2,1)} all-gather(bf16[64,1024]{1,0:T(8,128)(2,1)} %bitcast.47), channel_id=2, replica_groups={{0,256},{16,272},{32,288},{48,304},{64,320},{80,336},{96,352},{112,368}..., dimensions={0}, use_global_device_ids=true | all-gather | bytes 393216 | tf_op jit(solution)/shard_map/all_gather | solution.py:121
  15.5 0.0 all-gather.4.cloned.1.call-update
  15.5 0.7 iota_compare_fusion
  16.3 1.1 broadcast_select_fusion
  17.4 0.9 convolution_multiply_fusion.1
  18.3 0.0 copy-done
  18.3 0.0 copy-done.4
  18.3 0.6 fusion.6
  18.9 0.0 copy-start.3
  19.0 0.9 copy.11
  19.9 8.6 %all-to-all-start = ((f32[16,48,128]{2,1,0:T(8,128)}), f32[16,48,128]{2,1,0:T(8,128)S(1)}, u32[]{:S(2)}, u32[]{:S(2)}) async-start(f32[16,48,128]{2,1,0:T(8,128)} %bitcast), calls=%async_computation | async-start | bytes 786432 | tf_op jit(solution)/shard_map/all_to_all | solution.py:134
  28.5 2.1 %collective-permute-start = (bf16[768,128]{1,0:T(8,128)(2,1)S(1)}, bf16[768,128]{1,0:T(8,128)(2,1)S(1)}, u32[]{:S(2)}, u32[]{:S(2)}) collective-permute-start(bf16[768,128]{1,0:T(8,128)(2,1)S(1)} %broadcast_select_fusion), channel_id=1, source_target_pairs={{0,8},{1,9},{2,10},{3,11},{4,12},{5,13},{6,14},{7,15},{8,0},{9,1},... | collective-permute-start | bytes 589832 | tf_op jit(solution)/shard_map/ppermute | solution.py:135
  30.6 0.0 copy-done.3
  30.6 0.2 fusion.12
  30.8 7.7 %collective-permute-done = bf16[768,128]{1,0:T(8,128)(2,1)S(1)} collective-permute-done((bf16[768,128]{1,0:T(8,128)(2,1)S(1)}, bf16[768,128]{1,0:T(8,128)(2,1)S(1)}, u32[]{:S(2)}, u32[]{:S(2)}) %collective-permute-start) | collective-permute-done | bytes 196640 | tf_op jit(solution)/shard_map/ppermute | solution.py:135
  38.5 0.0 all-to-all-done
  38.6 1.9 %collective-permute-start.1 = (bf16[2,768,128]{2,1,0:T(8,128)(2,1)S(1)}, bf16[2,768,128]{2,1,0:T(8,128)(2,1)S(1)}, u32[]{:S(2)}, u32[]{:S(2)}) collective-permute-start(bf16[2,768,128]{2,1,0:T(8,128)(2,1)S(1)} %pad_maximum_fusion.2), channel_id=1, source_target_pairs={{0,1},{1,0},{2,3},{3,2},{4,5},{5,4},{6,7},{7,6},{8,9},{9,8},{10,11... | collective-permute-start | bytes 1179656 | tf_op jit(solution)/shard_map/ppermute | solution.py:142
  40.5 12.0 %all_to_all.20 = bf16[16,48,128]{2,1,0:T(8,128)(2,1)S(1)} all-to-all(bf16[16,48,128]{2,1,0:T(8,128)(2,1)S(1)} %broadcast_in_dim.16), channel_id=1, replica_groups=mesh['dp'=32,'tensor'=16] {'tensor'}, dimensions={0} | all-to-all | bytes 393216 | tf_op jit(solution)/shard_map/all_to_all | solution.py:141
  52.5 0.0 collective-permute-done.1
  52.5 0.2 fusion.1
  52.7 0.5 fusion
  53.3 0.7 pad_maximum_fusion.3
  53.9 0.1 pad_maximum_fusion.refs_0_
  54.0 0.0 copy-done.1
  54.0 0.0 copy-start.2
  54.0 2.0 %collective-permute-start.2 = (bf16[2,2,768,128]{3,2,1,0:T(8,128)(2,1)S(1)}, bf16[2,2,768,128]{3,2,1,0:T(8,128)(2,1)S(1)}, u32[]{:S(2)}, u32[]{:S(2)}) collective-permute-start(bf16[2,2,768,128]{3,2,1,0:T(8,128)(2,1)S(1)} %pad_maximum_fusion.refs_0_), channel_id=1, source_target_pairs={{0,2},{1,3},{2,4},{3,5},{4,6},{5,7},{6,0},{7,1},{8,10},{9,11},{10,... | collective-permute-start | bytes 2359304 | tf_op jit(solution)/shard_map/ppermute | solution.py:161
  56.0 5.1 %collective-permute-start.4 = (bf16[2,2,768,128]{3,2,1,0:T(8,128)(2,1)S(1)}, bf16[2,2,768,128]{3,2,1,0:T(8,128)(2,1)}, u32[]{:S(2)}, u32[]{:S(2)}) collective-permute-start(bf16[2,2,768,128]{3,2,1,0:T(8,128)(2,1)S(1)} %pad_maximum_fusion.refs_0_), channel_id=1, source_target_pairs={{0,6},{1,7},{2,0},{3,1},{4,2},{5,3},{6,4},{7,5},{8,14},{9,15},{10,... | collective-permute-start | bytes 2359304 | tf_op jit(solution)/shard_map/ppermute | solution.py:162
  61.1 12.5 %all-to-all-start.2 = ((bf16[16,8,640]{2,1,0:T(8,128)(2,1)}), bf16[16,8,640]{2,1,0:T(8,128)(2,1)S(1)}, u32[]{:S(2)}, u32[]{:S(2)}) async-start(bf16[16,8,640]{2,1,0:T(8,128)(2,1)} %bitcast.10), calls=%async_computation.2 | async-start | bytes 327680 | tf_op jit(solution)/shard_map/all_to_all | solution.py:159
  73.6 3.0 %collective-permute-done.2.refs_1_ = bf16[2,2,768,128]{3,2,1,0:T(8,128)(2,1)S(1)} collective-permute-done((bf16[2,2,768,128]{3,2,1,0:T(8,128)(2,1)S(1)}, bf16[2,2,768,128]{3,2,1,0:T(8,128)(2,1)S(1)}, u32[]{:S(2)}, u32[]{:S(2)}) %collective-permute-start.2) | collective-permute-done | bytes 786464 | tf_op jit(solution)/shard_map/ppermute | solution.py:161
  76.6 1.9 %collective-permute-start.5 = (bf16[2,2,768,128]{3,2,1,0:T(8,128)(2,1)S(1)}, bf16[2,2,768,128]{3,2,1,0:T(8,128)(2,1)}, u32[]{:S(2)}, u32[]{:S(2)}) collective-permute-start(bf16[2,2,768,128]{3,2,1,0:T(8,128)(2,1)S(1)} %collective-permute-done.2.refs_1_), channel_id=1, source_target_pairs={{0,2},{1,3},{2,4},{3,5},{4,6},{5,7},{6,0},{7,1},{8,10},{9,11},{10,... | collective-permute-start | bytes 2359304 | tf_op jit(solution)/shard_map/ppermute | solution.py:163
  78.5 11.8 %all-to-all-done.2 = bf16[16,8,640]{2,1,0:T(8,128)(2,1)S(1)} async-done(((bf16[16,8,640]{2,1,0:T(8,128)(2,1)}), bf16[16,8,640]{2,1,0:T(8,128)(2,1)S(1)}, u32[]{:S(2)}, u32[]{:S(2)}) %all-to-all-start.2) | async-done | bytes 163872 | tf_op jit(solution)/shard_map/all_to_all | solution.py:159
  90.3 4.1 %collective-permute-start.3 = (f32[8,640]{1,0:T(8,128)S(1)}, f32[8,640]{1,0:T(8,128)S(1)}, u32[]{:S(2)}, u32[]{:S(2)}) collective-permute-start(f32[8,640]{1,0:T(8,128)S(1)} %convert_reduce_fusion), channel_id=1, source_target_pairs={{0,256},{16,272},{32,288},{48,304},{64,320},{80,336},{96,352},{112... | collective-permute-start | bytes 61448 | tf_op jit(solution)/shard_map/ppermute | solution.py:167
  94.5 3.0 %collective-permute-done.3 = f32[8,640]{1,0:T(8,128)S(1)} collective-permute-done((f32[8,640]{1,0:T(8,128)S(1)}, f32[8,640]{1,0:T(8,128)S(1)}, u32[]{:S(2)}, u32[]{:S(2)}) %collective-permute-start.3) | collective-permute-done | bytes 20512 | tf_op jit(solution)/shard_map/ppermute | solution.py:167
  97.5 0.0 collective-permute-done.4.refs_3_
  97.5 0.7 broadcast_in_dim.28
  98.2 5.1 %all-to-all-start.3 = ((bf16[16,8,640]{2,1,0:T(8,128)(2,1)}), bf16[16,8,640]{2,1,0:T(8,128)(2,1)S(1)}, u32[]{:S(2)}, u32[]{:S(2)}) async-start(bf16[16,8,640]{2,1,0:T(8,128)(2,1)} %broadcast_in_dim.28), calls=%async_computation.3 | async-start | bytes 327680 | tf_op jit(solution)/shard_map/all_to_all | solution.py:170
  103.3 0.6 pad_add_fusion.place
  103.9 0.0 collective-permute-done.5.refs_2_
  103.9 0.2 all-gather.4.cloned.1.call-done
  104.1 0.0 copy-done.2
  104.1 0.0 copy-done.5
  104.1 8.2 %shard_map.85 = bf16[768,1024]{1,0:T(8,128)(2,1)} custom-call(s32[3]{0:T(128)} %pad_add_fusion.place, bf16[2,2,768,128]{3,2,1,0:T(8,128)(2,1)} %copy-done.2, bf16[2,2,768,128]{3,2,1,0:T(8,128)(2,1)} %copy-done.5, bf16[2,2,768,128]{3,2,1,0:T(8,128)(2,1)} %collective-permute-done.5.refs_2_, bf16[2,2,768,128]{3,2,1,0:T(8,128)(2,1)} %collective-permute-done.4.refs_3_, ...), custom_call_target="tpu_custom_call" | custom-call | flops 3321888768 | bytes 9437184 | tf_op jit(solution)/shard_map/pallas_call | solution.py:89
  112.2 5.6 %all-to-all-done.3 = bf16[16,8,640]{2,1,0:T(8,128)(2,1)S(1)} async-done(((bf16[16,8,640]{2,1,0:T(8,128)(2,1)}), bf16[16,8,640]{2,1,0:T(8,128)(2,1)S(1)}, u32[]{:S(2)}, u32[]{:S(2)}) %all-to-all-start.3) | async-done | bytes 163872 | tf_op jit(solution)/shard_map/all_to_all | solution.py:170
  117.9 0.7 slice.16
  118.6 0.6 slice_bitcast_fusion
  (11 shorter events, 0.2 us)
Async XLA Ops:
  7.2 11.1 %copy-start = (bf16[768,1024]{1,0:T(8,128)(2,1)S(1)}, bf16[768,1024]{1,0:T(8,128)(2,1)}, u32[]{:S(2)}) copy-start(bf16[768,1024]{1,0:T(8,128)(2,1)} %param.6) | copy-start | bytes 4718596
  7.2 11.1 %copy-start.4 = (bf16[1024,64]{0,1:T(8,128)(2,1)S(1)}, bf16[1024,64]{0,1:T(8,128)(2,1)}, u32[]{:S(2)}) copy-start(bf16[1024,64]{0,1:T(8,128)(2,1)} %param.9) | copy-start | bytes 393220
  7.2 96.9 %all-gather.4.cloned.1.call-start = ((), (), s32[]{:S(2)}) async-start(), calls=%async_computation.4 | async-start | bytes 4456448 | tf_op jit(solution)/shard_map/all_gather | solution.py:122
  18.9 11.7 %copy-start.3 = (bf16[768,128]{1,0:T(8,128)(2,1)S(1)}, bf16[768,128]{1,0:T(8,128)(2,1)}, u32[]{:S(2)}) copy-start(bf16[768,128]{1,0:T(8,128)(2,1)} %param.7) | copy-start | bytes 589828
  19.9 18.6 %all-to-all-start = ((f32[16,48,128]{2,1,0:T(8,128)}), f32[16,48,128]{2,1,0:T(8,128)S(1)}, u32[]{:S(2)}, u32[]{:S(2)}) async-start(f32[16,48,128]{2,1,0:T(8,128)} %bitcast), calls=%async_computation | async-start | bytes 786432 | tf_op jit(solution)/shard_map/all_to_all | solution.py:134
  28.5 9.9 %collective-permute-start = (bf16[768,128]{1,0:T(8,128)(2,1)S(1)}, bf16[768,128]{1,0:T(8,128)(2,1)S(1)}, u32[]{:S(2)}, u32[]{:S(2)}) collective-permute-start(bf16[768,128]{1,0:T(8,128)(2,1)S(1)} %broadcast_select_fusion), channel_id=1, source_target_pairs={{0,8},{1,9},{2,10},{3,11},{4,12},{5,13},{6,14},{7,15},{8,0},{9,1},... | collective-permute-start | bytes 589832 | tf_op jit(solution)/shard_map/ppermute | solution.py:135
  38.6 13.9 %collective-permute-start.1 = (bf16[2,768,128]{2,1,0:T(8,128)(2,1)S(1)}, bf16[2,768,128]{2,1,0:T(8,128)(2,1)S(1)}, u32[]{:S(2)}, u32[]{:S(2)}) collective-permute-start(bf16[2,768,128]{2,1,0:T(8,128)(2,1)S(1)} %pad_maximum_fusion.2), channel_id=1, source_target_pairs={{0,1},{1,0},{2,3},{3,2},{4,5},{5,4},{6,7},{7,6},{8,9},{9,8},{10,11... | collective-permute-start | bytes 1179656 | tf_op jit(solution)/shard_map/ppermute | solution.py:142
  52.5 1.5 %copy-start.1 = (bf16[16,48,128]{2,1,0:T(8,128)(2,1)}, bf16[16,48,128]{2,1,0:T(8,128)(2,1)S(1)}, u32[]{:S(2)}) copy-start(bf16[16,48,128]{2,1,0:T(8,128)(2,1)S(1)} %all_to_all.20) | copy-start | bytes 589828
  54.0 50.0 %copy-start.2 = (bf16[2,2,768,128]{3,2,1,0:T(8,128)(2,1)}, bf16[2,2,768,128]{3,2,1,0:T(8,128)(2,1)S(1)}, u32[]{:S(2)}) copy-start(bf16[2,2,768,128]{3,2,1,0:T(8,128)(2,1)S(1)} %pad_maximum_fusion.refs_0_) | copy-start | bytes 2359300
  54.0 22.5 %collective-permute-start.2 = (bf16[2,2,768,128]{3,2,1,0:T(8,128)(2,1)S(1)}, bf16[2,2,768,128]{3,2,1,0:T(8,128)(2,1)S(1)}, u32[]{:S(2)}, u32[]{:S(2)}) collective-permute-start(bf16[2,2,768,128]{3,2,1,0:T(8,128)(2,1)S(1)} %pad_maximum_fusion.refs_0_), channel_id=1, source_target_pairs={{0,2},{1,3},{2,4},{3,5},{4,6},{5,7},{6,0},{7,1},{8,10},{9,11},{10,... | collective-permute-start | bytes 2359304 | tf_op jit(solution)/shard_map/ppermute | solution.py:161
  56.0 41.5 %collective-permute-start.4 = (bf16[2,2,768,128]{3,2,1,0:T(8,128)(2,1)S(1)}, bf16[2,2,768,128]{3,2,1,0:T(8,128)(2,1)}, u32[]{:S(2)}, u32[]{:S(2)}) collective-permute-start(bf16[2,2,768,128]{3,2,1,0:T(8,128)(2,1)S(1)} %pad_maximum_fusion.refs_0_), channel_id=1, source_target_pairs={{0,6},{1,7},{2,0},{3,1},{4,2},{5,3},{6,4},{7,5},{8,14},{9,15},{10,... | collective-permute-start | bytes 2359304 | tf_op jit(solution)/shard_map/ppermute | solution.py:162
  61.1 29.2 %all-to-all-start.2 = ((bf16[16,8,640]{2,1,0:T(8,128)(2,1)}), bf16[16,8,640]{2,1,0:T(8,128)(2,1)S(1)}, u32[]{:S(2)}, u32[]{:S(2)}) async-start(bf16[16,8,640]{2,1,0:T(8,128)(2,1)} %bitcast.10), calls=%async_computation.2 | async-start | bytes 327680 | tf_op jit(solution)/shard_map/all_to_all | solution.py:159
  76.6 27.5 %copy-start.5 = (bf16[2,2,768,128]{3,2,1,0:T(8,128)(2,1)}, bf16[2,2,768,128]{3,2,1,0:T(8,128)(2,1)S(1)}, u32[]{:S(2)}) copy-start(bf16[2,2,768,128]{3,2,1,0:T(8,128)(2,1)S(1)} %collective-permute-done.2.refs_1_) | copy-start | bytes 2359300
  76.6 27.3 %collective-permute-start.5 = (bf16[2,2,768,128]{3,2,1,0:T(8,128)(2,1)S(1)}, bf16[2,2,768,128]{3,2,1,0:T(8,128)(2,1)}, u32[]{:S(2)}, u32[]{:S(2)}) collective-permute-start(bf16[2,2,768,128]{3,2,1,0:T(8,128)(2,1)S(1)} %collective-permute-done.2.refs_1_), channel_id=1, source_target_pairs={{0,2},{1,3},{2,4},{3,5},{4,6},{5,7},{6,0},{7,1},{8,10},{9,11},{10,... | collective-permute-start | bytes 2359304 | tf_op jit(solution)/shard_map/ppermute | solution.py:163
  90.3 7.2 %collective-permute-start.3 = (f32[8,640]{1,0:T(8,128)S(1)}, f32[8,640]{1,0:T(8,128)S(1)}, u32[]{:S(2)}, u32[]{:S(2)}) collective-permute-start(f32[8,640]{1,0:T(8,128)S(1)} %convert_reduce_fusion), channel_id=1, source_target_pairs={{0,256},{16,272},{32,288},{48,304},{64,320},{80,336},{96,352},{112... | collective-permute-start | bytes 61448 | tf_op jit(solution)/shard_map/ppermute | solution.py:167
  98.2 19.7 %all-to-all-start.3 = ((bf16[16,8,640]{2,1,0:T(8,128)(2,1)}), bf16[16,8,640]{2,1,0:T(8,128)(2,1)S(1)}, u32[]{:S(2)}, u32[]{:S(2)}) async-start(bf16[16,8,640]{2,1,0:T(8,128)(2,1)} %broadcast_in_dim.28), calls=%async_computation.3 | async-start | bytes 327680 | tf_op jit(solution)/shard_map/all_to_all | solution.py:170
Sparse Core Ops, SparseCore 0:
  15.6 88.3 all-gather.3

commit v5 on v4

--- a/solution.py
+++ b/solution.py
@@ -50,7 +50,7 @@
             copies.append(pltpu.make_async_copy(part, w_ref.at[r, k], w_sems.at[at]))
             copies.append(
                 pltpu.make_async_copy(
-                    blocks[r].at[k % 2, k // 2], g_ref.at[r, k], g_sems.at[at]
+                    blocks[r].at[k // 2, k % 2], g_ref.at[r, k], g_sems.at[at]
                 )
             )
     for copy in copies:
@@ -110,10 +110,42 @@
     )(place, *blocks, low_rows, w_all, down_t)
 
 
+def parts_kernel(lengths, me, hidden, kv_grad, down_t, up, masked, parts):
+    rows, slots = kv_grad.shape[0], kv_grad.shape[0] // lengths.shape[0]
+    for i in range(lengths.shape[0]):
+        at = pl.ds(i * slots, slots)
+        position = lax.broadcasted_iota(jnp.int32, (slots, 128), 0)
+        mine = jnp.where(position < lengths[i], kv_grad[at, :].astype(jnp.float32), 0.0)
+        masked[at, :] = mine.astype(masked.dtype)
+    up_mine = up[:, pl.ds(pl.multiple_of(me[0] * 128, 128), 128)]
+    both = jnp.concatenate(
+        [dot(hidden[...], down_t[...], 1, 1), 0.25 * dot(masked[...], up_mine, 1, 1)],
+        axis=1,
+    )
+    parts[...] = both.reshape(parts.shape)
+
+
+def low_parts(lengths, me, hidden, kv_grad, down_t, up):
+    rows = kv_grad.shape[0]
+    smem = pl.BlockSpec(memory_space=pltpu.SMEM)
+    whole = lambda a: pl.BlockSpec(a.shape, lambda i: (0,) * len(a.shape))
+    out_shape = (
+        jax.ShapeDtypeStruct((rows, 128), jnp.bfloat16),
+        jax.ShapeDtypeStruct((NT, rows // NT, 128), jnp.float32),
+    )
+    return pl.pallas_call(
+        parts_kernel,
+        grid=(1,),
+        in_specs=[smem, smem] + [whole(a) for a in (hidden, kv_grad, down_t, up)],
+        out_specs=tuple(whole(a) for a in out_shape),
+        out_shape=out_shape,
+        compiler_params=pltpu.CompilerParams(vmem_limit_bytes=58 * 1024 * 1024),
+    )(lengths, me, hidden, kv_grad, down_t, up)
+
+
 def per_device(hidden_in, kv_grad, frozen_kv, adapter_down, adapter_up, lengths):
     rows, features = hidden_in.shape
     local_seqs = lengths.shape[0]
-    slots = rows // local_seqs
     total_seqs = local_seqs * lax.axis_size("dp")
     me = lax.axis_index("tensor")
     place = jnp.stack([me // 8, me // 2 % NY, me % 2]).astype(jnp.int32)
@@ -121,25 +153,19 @@
     w_pair = lax.all_gather(frozen_kv.T, "dp", axis=0, axis_index_groups=XH_GROUPS)
     w_all = lax.all_gather(w_pair, "dp", axis=0, axis_index_groups=Z_GROUPS)
 
-    position = jnp.arange(slots, dtype=jnp.int32)
-    live = (position[None, :] < lengths[:, None]).reshape(rows, 1)
-    masked = jnp.where(live, kv_grad, jnp.zeros_like(kv_grad))
-
-    up_mine = lax.dynamic_slice_in_dim(adapter_up, me * 128, 128, axis=1)
-    parts = jnp.concatenate(
-        [dot(hidden_in, adapter_down, 1, 0), 0.25 * dot(masked, up_mine, 1, 1)], axis=1
-    )
-    parts = parts.reshape(NT, rows // NT, 128)
+    masked, parts = low_parts(
+        lengths, me.astype(jnp.int32).reshape(1), hidden_in, kv_grad, adapter_down.T, adapter_up
+    )
     parts, w_pair, to_swap = lax.optimization_barrier((parts, w_pair, masked))
     parts = lax.all_to_all(parts, "tensor", 0, 0)
-    swapped = lax.ppermute(to_swap, "tensor", XL_SWAP)
+    swapped = lax.ppermute(to_swap, "tensor", CORE_SWAP)
     parts, swapped = lax.optimization_barrier((parts, swapped))
     summed = parts.sum(axis=0).astype(jnp.bfloat16)
     spread = jnp.broadcast_to(summed[None], (NT,) + summed.shape)
     pair = jnp.stack([masked, swapped])
     spread, pair = lax.optimization_barrier((spread, pair))
     low_rows = lax.all_to_all(spread, "tensor", 0, 0).reshape(rows, 128)
-    pair_other = lax.ppermute(pair, "tensor", CORE_SWAP)
+    pair_other = lax.ppermute(pair, "tensor", XL_SWAP)
     low_rows, pair_other = lax.optimization_barrier((low_rows, pair_other))
     projected, coupled = low_rows[:, :64], low_rows[:, 64:]
 

time: 127 us -> 126 us (level)
  Pallas kernels: 8.17 us -> 11.2 us
  matrix products: 2.25 us -> 0.73 us
  waiting for transfers between devices: 31.2 us -> 29.9 us
    ppermute x2, waiting for transfers between devices: 7.67 us -> 1.48 us  [the longest x1 1.48 us: per_device(): swapped = lax.ppermute(to_swap, 'tensor', CORE_SWAP)]
    all_to_all x1, waiting for transfers between devices: 0.01 us -> 4.57 us  [per_device(): parts = lax.all_to_all(parts, 'tensor', 0, 0)]
    pallas_call x0 -> x1, Pallas kernels: none -> 3 us  [low_parts(): pl.pallas_call(parts_kernel, grid=(1,), in_specs=[smem, smem] + [whole(a)...]
    dot_general x4 -> x2, matrix products: 2.25 us -> 0.73 us  [dot(): lax.dot_general(left, right, (((left_dim,), (right_dim,)), ((), ())), pre...]
    ppermute x2, starting transfers between devices: 4 us -> 5.43 us  [the longest x1 3.39 us: per_device(): pair_other = lax.ppermute(pair, 'tensor', XL_SWAP)]
  transfers between devices with their start and end apart: 10 -> 10, of which waited for: 6 -> 7; matrix products, arithmetic and copies ran while one was open for 6% -> 3% of each run, Pallas kernels for 6% -> 9%
where the time goes in v5:
time: 126 us; the launch traced here: 125 us
  starting transfers between devices  44.2 us (35%)
  waiting for transfers between devices  29.9 us (24%)
  blocking collectives  20.4 us (16%)
  between operations  14.2 us (11%)
  Pallas kernels  11.2 us (9%)
  other arithmetic  2.43 us (2%)
  local copies, waits for them, and re-layouts  2.15 us (2%)
    all_to_all x1, starting transfers between devices, per_device(): grads = lax.all_to_all(grads, 'dp', 0, 0, axis_index_groups=Z_GROUPS)  12.6 us
    all_to_all x1, waiting for transfers between devices, per_device(): grads = lax.all_to_all(grads, 'dp', 0, 0, axis_index_groups=Z_GROUPS)  12.3 us
    all_to_all x1, blocking collectives, per_device(): low_rows = lax.all_to_all(spread, 'tensor', 0, 0).reshape(rows, 128)  12.3 us
    all_to_all x1, starting transfers between devices, per_device(): parts = lax.all_to_all(parts, 'tensor', 0, 0)  8.76 us
    pallas_call x1, Pallas kernels, input_gradient(): pl.pallas_call(grad_kernel, grid_spec=pltpu.PrefetchScalarGridSpec(num_sc...  8.17 us
    all_gather x1, blocking collectives, per_device(): lax.all_gather(frozen_kv.T, 'dp', axis=0, axis_index_groups=XH_GROUPS)  8.13 us
    ppermute x1, starting transfers between devices, per_device(): blocks += [lax.ppermute(block, 'tensor', y_shift(-1))]  5.05 us
    all_to_all x1, starting transfers between devices, per_device(): grads = lax.all_to_all(spread, 'dp', 0, 0, axis_index_groups=Z_GROUPS)  4.7 us
  transfers between devices with their start and end apart: 10, of which 7 were waited for; matrix products, arithmetic and copies ran while one was open for 3% of the time, Pallas kernels for 9%

profile of v5, /device:TPU:2, one launch (start us, length us, event | category | flops | bytes accessed | tf_op | source)
XLA Modules:
  0.0 125.2 jit_solution(12553325809560806584)
XLA Ops:
  7.2 0.0 all-gather.4.cloned.1.call-start
  7.2 8.1 %all-gather = bf16[128,1024]{1,0:T(8,128)(2,1)} all-gather(bf16[64,1024]{1,0:T(8,128)(2,1)} %bitcast.44), channel_id=2, replica_groups={{0,256},{16,272},{32,288},{48,304},{64,320},{80,336},{96,352},{112,368}..., dimensions={0}, use_global_device_ids=true | all-gather | bytes 393216 | tf_op jit(solution)/shard_map/all_gather | solution.py:153
  15.3 0.0 all-gather.4.cloned.1.call-update
  15.4 3.0 %shard_map.85 = (bf16[768,128]{1,0:T(8,128)(2,1)}, f32[16,48,128]{2,1,0:T(8,128)}) custom-call(s32[2]{0:T(128)} %lengths.1, s32[1]{0:T(128)} %bitcast.me, bf16[768,1024]{1,0:T(8,128)(2,1)} %hidden.1, bf16[768,128]{1,0:T(8,128)(2,1)} %kv_grad.1, bf16[64,1024]{1,0:T(8,128)(2,1)} %bitcast.45, bf16[64,2048]{1,0:T(8,128)(2,1)} %up.1), custom_call_target="tpu_custom_call" | custom-call | tf_op jit(solution)/shard_map/pallas_call | solution.py:136
  18.4 0.0 copy-start.3
  18.4 0.0 copy-start
  18.4 8.8 %all-to-all-start = ((f32[16,48,128]{2,1,0:T(8,128)}), f32[16,48,128]{2,1,0:T(8,128)S(1)}, u32[]{:S(2)}, u32[]{:S(2)}) async-start(f32[16,48,128]{2,1,0:T(8,128)} %get-tuple-element.24), calls=%async_computation | async-start | bytes 786432 | tf_op jit(solution)/shard_map/all_to_all | solution.py:160
  27.1 2.0 %collective-permute-start = (bf16[768,128]{1,0:T(8,128)(2,1)}, bf16[768,128]{1,0:T(8,128)(2,1)S(1)}, u32[]{:S(2)}, u32[]{:S(2)}) collective-permute-start(bf16[768,128]{1,0:T(8,128)(2,1)} %get-tuple-element.25), channel_id=1, source_target_pairs={{0,1},{1,0},{2,3},{3,2},{4,5},{5,4},{6,7},{7,6},{8,9},{9,8},{10,11... | collective-permute-start | bytes 589832 | tf_op jit(solution)/shard_map/ppermute | solution.py:161
  29.2 1.5 %collective-permute-done = bf16[768,128]{1,0:T(8,128)(2,1)S(1)} collective-permute-done((bf16[768,128]{1,0:T(8,128)(2,1)}, bf16[768,128]{1,0:T(8,128)(2,1)S(1)}, u32[]{:S(2)}, u32[]{:S(2)}) %collective-permute-start) | collective-permute-done | bytes 196640 | tf_op jit(solution)/shard_map/ppermute | solution.py:161
  30.7 4.6 %all-to-all-done = f32[16,48,128]{2,1,0:T(8,128)S(1)} async-done(((f32[16,48,128]{2,1,0:T(8,128)}), f32[16,48,128]{2,1,0:T(8,128)S(1)}, u32[]{:S(2)}, u32[]{:S(2)}) %all-to-all-start) | async-done | bytes 393248 | tf_op jit(solution)/shard_map/all_to_all | solution.py:160
  35.3 1.0 pad_maximum_fusion.1
  36.3 3.4 %collective-permute-start.1 = (bf16[2,768,128]{2,1,0:T(8,128)(2,1)S(1)}, bf16[2,768,128]{2,1,0:T(8,128)(2,1)S(1)}, u32[]{:S(2)}, u32[]{:S(2)}) collective-permute-start(bf16[2,768,128]{2,1,0:T(8,128)(2,1)S(1)} %pad_maximum_fusion.1), channel_id=1, source_target_pairs={{0,8},{1,9},{2,10},{3,11},{4,12},{5,13},{6,14},{7,15},{8,0},{9,1},... | collective-permute-start | bytes 1179656 | tf_op jit(solution)/shard_map/ppermute | solution.py:168
  39.7 12.3 %all_to_all.20 = bf16[16,48,128]{2,1,0:T(8,128)(2,1)S(1)} all-to-all(bf16[16,48,128]{2,1,0:T(8,128)(2,1)S(1)} %broadcast_in_dim.4), channel_id=1, replica_groups=mesh['dp'=32,'tensor'=16] {'tensor'}, dimensions={0} | all-to-all | bytes 393216 | tf_op jit(solution)/shard_map/all_to_all | solution.py:167
  52.0 0.0 copy-start.1
  52.0 0.0 collective-permute-done.1
  52.0 0.0 copy-done.3
  52.0 0.2 fusion.1
  52.2 0.0 copy-done
  52.2 0.5 fusion
  52.8 0.7 pad_maximum_fusion.2
  53.4 0.1 pad_maximum_fusion.refs_0_
  53.5 0.0 copy-done.1
  53.5 0.0 copy-start.2
  53.5 2.0 %collective-permute-start.2 = (bf16[2,2,768,128]{3,2,1,0:T(8,128)(2,1)S(1)}, bf16[2,2,768,128]{3,2,1,0:T(8,128)(2,1)S(1)}, u32[]{:S(2)}, u32[]{:S(2)}) collective-permute-start(bf16[2,2,768,128]{3,2,1,0:T(8,128)(2,1)S(1)} %pad_maximum_fusion.refs_0_), channel_id=1, source_target_pairs={{0,2},{1,3},{2,4},{3,5},{4,6},{5,7},{6,0},{7,1},{8,10},{9,11},{10,... | collective-permute-start | bytes 2359304 | tf_op jit(solution)/shard_map/ppermute | solution.py:187
  55.5 5.0 %collective-permute-start.4 = (bf16[2,2,768,128]{3,2,1,0:T(8,128)(2,1)S(1)}, bf16[2,2,768,128]{3,2,1,0:T(8,128)(2,1)S(1)}, u32[]{:S(2)}, u32[]{:S(2)}) collective-permute-start(bf16[2,2,768,128]{3,2,1,0:T(8,128)(2,1)S(1)} %pad_maximum_fusion.refs_0_), channel_id=1, source_target_pairs={{0,6},{1,7},{2,0},{3,1},{4,2},{5,3},{6,4},{7,5},{8,14},{9,15},{10,... | collective-permute-start | bytes 2359304 | tf_op jit(solution)/shard_map/ppermute | solution.py:188
  60.6 12.6 %all-to-all-start.2 = ((bf16[16,8,640]{2,1,0:T(8,128)(2,1)}), bf16[16,8,640]{2,1,0:T(8,128)(2,1)S(1)}, u32[]{:S(2)}, u32[]{:S(2)}) async-start(bf16[16,8,640]{2,1,0:T(8,128)(2,1)} %bitcast.11), calls=%async_computation.2 | async-start | bytes 327680 | tf_op jit(solution)/shard_map/all_to_all | solution.py:185
  73.2 2.6 %collective-permute-done.2.refs_1_ = bf16[2,2,768,128]{3,2,1,0:T(8,128)(2,1)S(1)} collective-permute-done((bf16[2,2,768,128]{3,2,1,0:T(8,128)(2,1)S(1)}, bf16[2,2,768,128]{3,2,1,0:T(8,128)(2,1)S(1)}, u32[]{:S(2)}, u32[]{:S(2)}) %collective-permute-start.2) | collective-permute-done | bytes 786464 | tf_op jit(solution)/shard_map/ppermute | solution.py:187
  75.8 0.0 copy-start.4
  75.8 1.9 %collective-permute-start.5 = (bf16[2,2,768,128]{3,2,1,0:T(8,128)(2,1)S(1)}, bf16[2,2,768,128]{3,2,1,0:T(8,128)(2,1)S(1)}, u32[]{:S(2)}, u32[]{:S(2)}) collective-permute-start(bf16[2,2,768,128]{3,2,1,0:T(8,128)(2,1)S(1)} %collective-permute-done.2.refs_1_), channel_id=1, source_target_pairs={{0,2},{1,3},{2,4},{3,5},{4,6},{5,7},{6,0},{7,1},{8,10},{9,11},{10,... | collective-permute-start | bytes 2359304 | tf_op jit(solution)/shard_map/ppermute | solution.py:189
  77.7 12.3 %all-to-all-done.2 = bf16[16,8,640]{2,1,0:T(8,128)(2,1)S(1)} async-done(((bf16[16,8,640]{2,1,0:T(8,128)(2,1)}), bf16[16,8,640]{2,1,0:T(8,128)(2,1)S(1)}, u32[]{:S(2)}, u32[]{:S(2)}) %all-to-all-start.2) | async-done | bytes 163872 | tf_op jit(solution)/shard_map/all_to_all | solution.py:185
  90.0 3.7 %collective-permute-start.3 = (f32[8,640]{1,0:T(8,128)S(1)}, f32[8,640]{1,0:T(8,128)S(1)}, u32[]{:S(2)}, u32[]{:S(2)}) collective-permute-start(f32[8,640]{1,0:T(8,128)S(1)} %convert_reduce_fusion), channel_id=1, source_target_pairs={{0,256},{16,272},{32,288},{48,304},{64,320},{80,336},{96,352},{112... | collective-permute-start | bytes 61448 | tf_op jit(solution)/shard_map/ppermute | solution.py:193
  93.8 3.4 %collective-permute-done.3 = f32[8,640]{1,0:T(8,128)S(1)} collective-permute-done((f32[8,640]{1,0:T(8,128)S(1)}, f32[8,640]{1,0:T(8,128)S(1)}, u32[]{:S(2)}, u32[]{:S(2)}) %collective-permute-start.3) | collective-permute-done | bytes 20512 | tf_op jit(solution)/shard_map/ppermute | solution.py:193
  97.2 0.0 collective-permute-done.4.refs_3_
  97.2 0.0 copy-start.5
  97.2 0.7 broadcast_in_dim.5
  98.0 4.7 %all-to-all-start.3 = ((bf16[16,8,640]{2,1,0:T(8,128)(2,1)}), bf16[16,8,640]{2,1,0:T(8,128)(2,1)S(1)}, u32[]{:S(2)}, u32[]{:S(2)}) async-start(bf16[16,8,640]{2,1,0:T(8,128)(2,1)} %broadcast_in_dim.5), calls=%async_computation.3 | async-start | bytes 327680 | tf_op jit(solution)/shard_map/all_to_all | solution.py:196
  102.7 0.6 pad_add_fusion.place
  103.3 0.0 collective-permute-done.5.refs_2_
  103.3 0.0 copy-start.6
  103.3 1.2 all-gather.4.cloned.1.call-done
  104.5 0.0 copy-done.2
  104.5 0.0 copy-done.4
  104.5 0.0 copy-done.5
  104.5 0.0 copy-done.6
  104.5 8.2 %shard_map.86 = bf16[768,1024]{1,0:T(8,128)(2,1)} custom-call(s32[3]{0:T(128)} %pad_add_fusion.place, bf16[2,2,768,128]{3,2,1,0:T(8,128)(2,1)} %copy-done.2, bf16[2,2,768,128]{3,2,1,0:T(8,128)(2,1)} %copy-done.4, bf16[2,2,768,128]{3,2,1,0:T(8,128)(2,1)} %copy-done.6, bf16[2,2,768,128]{3,2,1,0:T(8,128)(2,1)} %copy-done.5, bf16[768,128]{1,0:T(8,128)(2,1)} %bitcast.36, ...), custom_call_target="tpu_custom_call" | custom-call | flops 3321888768 | bytes 9437184 | tf_op jit(solution)/shard_map/pallas_call | solution.py:89
  112.7 4.3 %all-to-all-done.3 = bf16[16,8,640]{2,1,0:T(8,128)(2,1)S(1)} async-done(((bf16[16,8,640]{2,1,0:T(8,128)(2,1)}), bf16[16,8,640]{2,1,0:T(8,128)(2,1)S(1)}, u32[]{:S(2)}, u32[]{:S(2)}) %all-to-all-start.3) | async-done | bytes 163872 | tf_op jit(solution)/shard_map/all_to_all | solution.py:196
  117.0 0.7 slice.16
  117.8 0.6 slice_bitcast_fusion
  (6 shorter events, 0.1 us)
Async XLA Ops:
  7.2 97.3 %all-gather.4.cloned.1.call-start = ((), (), s32[]{:S(2)}) async-start(), calls=%async_computation.4 | async-start | bytes 4456448 | tf_op jit(solution)/shard_map/all_gather | solution.py:154
  18.4 33.6 %copy-start.3 = (bf16[768,128]{1,0:T(8,128)(2,1)S(1)}, bf16[768,128]{1,0:T(8,128)(2,1)}, u32[]{:S(2)}) copy-start(bf16[768,128]{1,0:T(8,128)(2,1)} %get-tuple-element.25) | copy-start | bytes 589828
  18.4 33.9 %copy-start = (bf16[768,1024]{1,0:T(8,128)(2,1)S(1)}, bf16[768,1024]{1,0:T(8,128)(2,1)}, u32[]{:S(2)}) copy-start(bf16[768,1024]{1,0:T(8,128)(2,1)} %hidden.1) | copy-start | bytes 4718596
  18.4 16.9 %all-to-all-start = ((f32[16,48,128]{2,1,0:T(8,128)}), f32[16,48,128]{2,1,0:T(8,128)S(1)}, u32[]{:S(2)}, u32[]{:S(2)}) async-start(f32[16,48,128]{2,1,0:T(8,128)} %get-tuple-element.24), calls=%async_computation | async-start | bytes 786432 | tf_op jit(solution)/shard_map/all_to_all | solution.py:160
  27.1 3.5 %collective-permute-start = (bf16[768,128]{1,0:T(8,128)(2,1)}, bf16[768,128]{1,0:T(8,128)(2,1)S(1)}, u32[]{:S(2)}, u32[]{:S(2)}) collective-permute-start(bf16[768,128]{1,0:T(8,128)(2,1)} %get-tuple-element.25), channel_id=1, source_target_pairs={{0,1},{1,0},{2,3},{3,2},{4,5},{5,4},{6,7},{7,6},{8,9},{9,8},{10,11... | collective-permute-start | bytes 589832 | tf_op jit(solution)/shard_map/ppermute | solution.py:161
  36.3 15.7 %collective-permute-start.1 = (bf16[2,768,128]{2,1,0:T(8,128)(2,1)S(1)}, bf16[2,768,128]{2,1,0:T(8,128)(2,1)S(1)}, u32[]{:S(2)}, u32[]{:S(2)}) collective-permute-start(bf16[2,768,128]{2,1,0:T(8,128)(2,1)S(1)} %pad_maximum_fusion.1), channel_id=1, source_target_pairs={{0,8},{1,9},{2,10},{3,11},{4,12},{5,13},{6,14},{7,15},{8,0},{9,1},... | collective-permute-start | bytes 1179656 | tf_op jit(solution)/shard_map/ppermute | solution.py:168
  52.0 1.5 %copy-start.1 = (bf16[16,48,128]{2,1,0:T(8,128)(2,1)}, bf16[16,48,128]{2,1,0:T(8,128)(2,1)S(1)}, u32[]{:S(2)}) copy-start(bf16[16,48,128]{2,1,0:T(8,128)(2,1)S(1)} %all_to_all.20) | copy-start | bytes 589828
  53.5 51.0 %copy-start.2 = (bf16[2,2,768,128]{3,2,1,0:T(8,128)(2,1)}, bf16[2,2,768,128]{3,2,1,0:T(8,128)(2,1)S(1)}, u32[]{:S(2)}) copy-start(bf16[2,2,768,128]{3,2,1,0:T(8,128)(2,1)S(1)} %pad_maximum_fusion.refs_0_) | copy-start | bytes 2359300
  53.5 22.2 %collective-permute-start.2 = (bf16[2,2,768,128]{3,2,1,0:T(8,128)(2,1)S(1)}, bf16[2,2,768,128]{3,2,1,0:T(8,128)(2,1)S(1)}, u32[]{:S(2)}, u32[]{:S(2)}) collective-permute-start(bf16[2,2,768,128]{3,2,1,0:T(8,128)(2,1)S(1)} %pad_maximum_fusion.refs_0_), channel_id=1, source_target_pairs={{0,2},{1,3},{2,4},{3,5},{4,6},{5,7},{6,0},{7,1},{8,10},{9,11},{10,... | collective-permute-start | bytes 2359304 | tf_op jit(solution)/shard_map/ppermute | solution.py:187
  55.5 41.7 %collective-permute-start.4 = (bf16[2,2,768,128]{3,2,1,0:T(8,128)(2,1)S(1)}, bf16[2,2,768,128]{3,2,1,0:T(8,128)(2,1)S(1)}, u32[]{:S(2)}, u32[]{:S(2)}) collective-permute-start(bf16[2,2,768,128]{3,2,1,0:T(8,128)(2,1)S(1)} %pad_maximum_fusion.refs_0_), channel_id=1, source_target_pairs={{0,6},{1,7},{2,0},{3,1},{4,2},{5,3},{6,4},{7,5},{8,14},{9,15},{10,... | collective-permute-start | bytes 2359304 | tf_op jit(solution)/shard_map/ppermute | solution.py:188
  60.6 29.4 %all-to-all-start.2 = ((bf16[16,8,640]{2,1,0:T(8,128)(2,1)}), bf16[16,8,640]{2,1,0:T(8,128)(2,1)S(1)}, u32[]{:S(2)}, u32[]{:S(2)}) async-start(bf16[16,8,640]{2,1,0:T(8,128)(2,1)} %bitcast.11), calls=%async_computation.2 | async-start | bytes 327680 | tf_op jit(solution)/shard_map/all_to_all | solution.py:185
  75.8 28.7 %copy-start.4 = (bf16[2,2,768,128]{3,2,1,0:T(8,128)(2,1)}, bf16[2,2,768,128]{3,2,1,0:T(8,128)(2,1)S(1)}, u32[]{:S(2)}) copy-start(bf16[2,2,768,128]{3,2,1,0:T(8,128)(2,1)S(1)} %collective-permute-done.2.refs_1_) | copy-start | bytes 2359300
  75.8 27.5 %collective-permute-start.5 = (bf16[2,2,768,128]{3,2,1,0:T(8,128)(2,1)S(1)}, bf16[2,2,768,128]{3,2,1,0:T(8,128)(2,1)S(1)}, u32[]{:S(2)}, u32[]{:S(2)}) collective-permute-start(bf16[2,2,768,128]{3,2,1,0:T(8,128)(2,1)S(1)} %collective-permute-done.2.refs_1_), channel_id=1, source_target_pairs={{0,2},{1,3},{2,4},{3,5},{4,6},{5,7},{6,0},{7,1},{8,10},{9,11},{10,... | collective-permute-start | bytes 2359304 | tf_op jit(solution)/shard_map/ppermute | solution.py:189
  90.0 7.2 %collective-permute-start.3 = (f32[8,640]{1,0:T(8,128)S(1)}, f32[8,640]{1,0:T(8,128)S(1)}, u32[]{:S(2)}, u32[]{:S(2)}) collective-permute-start(f32[8,640]{1,0:T(8,128)S(1)} %convert_reduce_fusion), channel_id=1, source_target_pairs={{0,256},{16,272},{32,288},{48,304},{64,320},{80,336},{96,352},{112... | collective-permute-start | bytes 61448 | tf_op jit(solution)/shard_map/ppermute | solution.py:193
  97.2 7.3 %copy-start.5 = (bf16[2,2,768,128]{3,2,1,0:T(8,128)(2,1)}, bf16[2,2,768,128]{3,2,1,0:T(8,128)(2,1)S(1)}, u32[]{:S(2)}) copy-start(bf16[2,2,768,128]{3,2,1,0:T(8,128)(2,1)S(1)} %collective-permute-done.4.refs_3_) | copy-start | bytes 2359300
  98.0 19.0 %all-to-all-start.3 = ((bf16[16,8,640]{2,1,0:T(8,128)(2,1)}), bf16[16,8,640]{2,1,0:T(8,128)(2,1)S(1)}, u32[]{:S(2)}, u32[]{:S(2)}) async-start(bf16[16,8,640]{2,1,0:T(8,128)(2,1)} %broadcast_in_dim.5), calls=%async_computation.3 | async-start | bytes 327680 | tf_op jit(solution)/shard_map/all_to_all | solution.py:196
  103.3 1.2 copy-start.6
Sparse Core Ops, SparseCore 0:
  15.5 88.9 all-gather.3
